TPU v7x, 32 devices: a whole 2x2x4 slice. The times are simulated.
32 devices in a mesh: layer: 4 (over z), latent: 8 (over y, x, core).
Axes of the slice: x: 2, y: 2, z: 4, core: 2. Of those that a mesh axis runs over, the one named last changes fastest.
Arguments:
- resid: bfloat16 [4, 256, 4096], P('layer', 'latent'), may hold values from -6 to 6
- mlp_out: bfloat16 [4, 256, 4096], P('layer', 'latent'), may hold values from -6 to 6
- enc_w: bfloat16 [4, 4096, 4096], P('layer', None, 'latent'), may hold values from -0.09375 to 0.09375
- enc_b: float32 [4, 4096], P('layer', 'latent'), may hold values from -3 to 3
- dec_w: bfloat16 [4, 4, 4096, 4096], P('layer', None, 'latent'), may hold values from -0.046875 to 0.046875
Outputs:
- error: bfloat16 [4, 256, 4096], P('layer', 'latent')
All inputs are finite; a program needn't handle non-finite values.
Results may differ from a plain program's by a relative error of at most 0.0034.
Values may be sent and summed in bfloat16 or wider, within the bound.
No kernel may reach another device: no remote copies, remote signals or barrier semaphores. Data moves between devices by JAX's collectives and lax.ppermute only.
A program may use at most 128 MiB of HBM per device.

v0:
```python
import jax
import jax.numpy as jnp
from jax import lax
from jax.sharding import PartitionSpec as P


def shifted(shard, axis, by):
    peers = lax.axis_size(axis)
    pairs = [(i, i + by) for i in range(peers) if 0 <= i + by < peers]
    return lax.ppermute(shard, axis, pairs)


def body(resid, mlp_out, enc_w, enc_b, dec_w):
    target = lax.axis_index("layer")
    layer_count = lax.axis_size("layer")
    weights = dec_w[0]
    encoder = enc_w[0]
    bias = enc_b[0]
    pre = (
        jnp.dot(
            lax.all_gather(resid[0], "latent", axis=0, tiled=True),
            encoder,
            preferred_element_type=jnp.float32,
        )
        + bias
    )
    own_latents = jnp.maximum(pre, 0.0).astype(jnp.bfloat16)

    def decode_add(recon, block, source):

        def added(value):
            chosen = lax.dynamic_index_in_dim(weights, source, 0, keepdims=False)
            return value + jnp.dot(block, chosen, preferred_element_type=jnp.float32)

        return lax.cond(
            jnp.logical_and(source >= 0, source <= target), added, lambda value: value, recon
        )

    empty = jnp.zeros((own_latents.shape[0], weights.shape[2]), jnp.float32)
    recon = decode_add(empty, own_latents, target)
    carried = own_latents
    for step in range(1, layer_count):
        carried = shifted(carried, "layer", 1)
        recon = decode_add(recon, carried, target - step)
    mine = lax.psum_scatter(recon, "latent", scatter_dimension=0, tiled=True)
    return (mlp_out[0].astype(jnp.float32) - mine).astype(jnp.bfloat16)[None]


def solution(mesh):
    return jax.shard_map(
        body,
        mesh=mesh,
        in_specs=(
            P("layer", "latent", None),
            P("layer", "latent", None),
            P("layer", None, "latent"),
            P("layer", "latent"),
            P("layer", None, "latent", None),
        ),
        out_specs=P("layer", "latent", None),
        check_vma=False,
    )
```

profile of v0, /device:TPU:0, one launch (start us, length us, event | category | flops | bytes accessed | tf_op | source)
XLA Modules:
  0.0 156.9 jit_solution(7871437648156316851)
XLA Ops:
  6.5 0.0 all-gather.3.cloned.1.call-start
  6.5 0.7 all-gather.3.cloned.1.call-update
  7.3 0.0 reduce-scatter.2.cloned.1.call-start
  7.3 32.6 %all-gather.3.cloned.1.call-done = bf16[1,256,4096]{2,1,0:T(8,128)(2,1)} async-done(((bf16[1,32,4096]{2,1,0:T(8,128)(2,1)}), bf16[1,256,4096]{2,1,0:T(8,128)(2,1)}) %all-gather.3.cloned.1.call-update) | async-done | bytes 2097168 | tf_op jit(solution)/shard_map/all_gather | solution.py:21
  39.9 4.1 %fusion.28 = bf16[256,512]{1,0:T(8,128)(2,1)S(1)} fusion(bf16[1,4096,512]{2,1,0:T(8,128)(2,1)} %param.15, bf16[1,256,4096]{2,1,0:T(8,128)(2,1)} %all-gather.3.cloned.1.call-done, f32[512]{0:T(512)} %bitcast.59), kind=kOutput, calls=%fused_computation.24 | convolution fusion | flops 1074135040 | bytes 6555648 | tf_op jit(solution)/shard_map/dot_general | solution.py:20
  44.0 3.4 %collective-permute-start = (bf16[256,512]{1,0:T(8,128)(2,1)S(1)}, bf16[256,512]{1,0:T(8,128)(2,1)S(1)}, u32[]{:S(2)}, u32[]{:S(2)}) collective-permute-start(bf16[256,512]{1,0:T(8,128)(2,1)S(1)} %fusion.28), channel_id=1, source_target_pairs={{0,8},{8,16},{16,24},{1,9},{9,17},{17,25},{2,10},{10,18},{18,26},{... | collective-permute-start | bytes 786440 | tf_op jit(solution)/shard_map/ppermute | solution.py:10
  47.4 6.0 %collective-permute-done = bf16[256,512]{1,0:T(8,128)(2,1)S(1)} collective-permute-done((bf16[256,512]{1,0:T(8,128)(2,1)S(1)}, bf16[256,512]{1,0:T(8,128)(2,1)S(1)}, u32[]{:S(2)}, u32[]{:S(2)}) %collective-permute-start) | collective-permute-done | bytes 262176 | tf_op jit(solution)/shard_map/ppermute | solution.py:10
  53.4 5.1 %collective-permute-start.1 = (bf16[256,512]{1,0:T(8,128)(2,1)S(1)}, bf16[256,512]{1,0:T(8,128)(2,1)}, u32[]{:S(2)}, u32[]{:S(2)}) collective-permute-start(bf16[256,512]{1,0:T(8,128)(2,1)S(1)} %collective-permute-done), channel_id=1, source_target_pairs={{0,8},{8,16},{16,24},{1,9},{9,17},{17,25},{2,10},{10,18},{18,26},{... | collective-permute-start | bytes 786440 | tf_op jit(solution)/shard_map/ppermute | solution.py:10
  58.4 4.5 %collective-permute-done.1 = bf16[256,512]{1,0:T(8,128)(2,1)} collective-permute-done((bf16[256,512]{1,0:T(8,128)(2,1)S(1)}, bf16[256,512]{1,0:T(8,128)(2,1)}, u32[]{:S(2)}, u32[]{:S(2)}) %collective-permute-start.1) | collective-permute-done | bytes 262176 | tf_op jit(solution)/shard_map/ppermute | solution.py:10
  62.9 4.5 %collective-permute-start.2 = (bf16[256,512]{1,0:T(8,128)(2,1)}, bf16[256,512]{1,0:T(8,128)(2,1)S(1)}, u32[]{:S(2)}, u32[]{:S(2)}) collective-permute-start(bf16[256,512]{1,0:T(8,128)(2,1)} %collective-permute-done.1), channel_id=1, source_target_pairs={{0,8},{8,16},{16,24},{1,9},{9,17},{17,25},{2,10},{10,18},{18,26},{... | collective-permute-start | bytes 786440 | tf_op jit(solution)/shard_map/ppermute | solution.py:10
  67.4 5.5 %conditional.4 = (f32[256,4096]{0,1:T(8,128)}) conditional(s32[]{:T(128)} %convert_element_type.29, () %tuple.29, (s32[]{:T(128)}, bf16[4,512,4096]{2,1,0:T(8,128)(2,1)}, bf16[256,512]{1,0:T(8,128)(2,1)S(1)}) %tuple.46), branch_computations={%region_0.0_spmd, %region_1.2_spmd} | conditional | flops 1073741824 | bytes 8650798 | solution.py:35
  67.4 5.5 %convolution_bitcast_fusion = f32[256,4096]{0,1:T(8,128)} fusion(bf16[256,512]{1,0:T(8,128)(2,1)S(1)} %get-tuple-element.52, bf16[4,512,4096]{2,1,0:T(8,128)(2,1)} %get-tuple-element.50, s32[]{:T(128)S(6)} %select_n.9), kind=kOutput, calls=%fused_computation | convolution fusion | flops 1073741824 | bytes 8650756 | tf_op jit(solution)/shard_map/cond/branch_1_fun/dot_general | solution.py:33
  72.9 0.0 collective-permute-done.2
  72.9 5.6 %copy.6 = f32[256,4096]{1,0:T(8,128)} copy(f32[256,4096]{0,1:T(8,128)} %get-tuple-element.68) | data formatting | bytes 8388608 | tf_op jit(solution)/shard_map/cond | solution.py:35
  78.5 0.0 copy-start
  78.5 0.0 reduce-scatter.2.cloned.1.call-update
  78.5 69.7 %reduce-scatter.2.cloned.1.call-done = f32[32,4096]{1,0:T(8,128)} async-done(((f32[256,4096]{1,0:T(8,128)}), f32[32,4096]{1,0:T(8,128)}) %reduce-scatter.2.cloned.1.call-update) | async-done | bytes 524304 | tf_op jit(solution)/shard_map/reduce_scatter | solution.py:45
  148.2 0.0 copy-done
  148.2 1.8 %fusion.34 = bf16[1,32,4096]{2,1,0:T(8,128)(2,1)} fusion(f32[32,4096]{1,0:T(8,128)} %reduce-scatter.2.cloned.1.call-done, bf16[1,32,4096]{2,1,0:T(8,128)(2,1)S(1)} %copy-done), kind=kLoop, calls=%fused_computation.27 | loop fusion | flops 393216 | bytes 1048576 | tf_op jit(solution)/shard_map/broadcast_in_dim | solution.py:46
  (3 shorter events, 0.0 us)
Async XLA Ops:
  6.5 33.3 %all-gather.3.cloned.1.call-start = ((), (), s32[]{:S(2)}) async-start(), calls=%async_computation.2 | async-start | bytes 2359296 | tf_op jit(solution)/shard_map/all_gather | solution.py:21
  7.3 141.0 %reduce-scatter.2.cloned.1.call-start = ((), (), s32[]{:S(2)}) async-start(), calls=%async_computation.1 | async-start | bytes 4718592 | tf_op jit(solution)/shard_map/reduce_scatter | solution.py:45
  44.0 9.4 %collective-permute-start = (bf16[256,512]{1,0:T(8,128)(2,1)S(1)}, bf16[256,512]{1,0:T(8,128)(2,1)S(1)}, u32[]{:S(2)}, u32[]{:S(2)}) collective-permute-start(bf16[256,512]{1,0:T(8,128)(2,1)S(1)} %fusion.28), channel_id=1, source_target_pairs={{0,8},{8,16},{16,24},{1,9},{9,17},{17,25},{2,10},{10,18},{18,26},{... | collective-permute-start | bytes 786440 | tf_op jit(solution)/shard_map/ppermute | solution.py:10
  53.4 9.5 %collective-permute-start.1 = (bf16[256,512]{1,0:T(8,128)(2,1)S(1)}, bf16[256,512]{1,0:T(8,128)(2,1)}, u32[]{:S(2)}, u32[]{:S(2)}) collective-permute-start(bf16[256,512]{1,0:T(8,128)(2,1)S(1)} %collective-permute-done), channel_id=1, source_target_pairs={{0,8},{8,16},{16,24},{1,9},{9,17},{17,25},{2,10},{10,18},{18,26},{... | collective-permute-start | bytes 786440 | tf_op jit(solution)/shard_map/ppermute | solution.py:10
  62.9 10.0 %collective-permute-start.2 = (bf16[256,512]{1,0:T(8,128)(2,1)}, bf16[256,512]{1,0:T(8,128)(2,1)S(1)}, u32[]{:S(2)}, u32[]{:S(2)}) collective-permute-start(bf16[256,512]{1,0:T(8,128)(2,1)} %collective-permute-done.1), channel_id=1, source_target_pairs={{0,8},{8,16},{16,24},{1,9},{9,17},{17,25},{2,10},{10,18},{18,26},{... | collective-permute-start | bytes 786440 | tf_op jit(solution)/shard_map/ppermute | solution.py:10
  78.5 69.7 %copy-start = (bf16[1,32,4096]{2,1,0:T(8,128)(2,1)S(1)}, bf16[1,32,4096]{2,1,0:T(8,128)(2,1)}, u32[]{:S(2)}) copy-start(bf16[1,32,4096]{2,1,0:T(8,128)(2,1)} %param.14) | copy-start | bytes 786436
Sparse Core Ops, SparseCore 0:
  9.2 30.5 all-gather.2
  78.7 69.5 reduce-scatter.1
where the time goes:
time: 157 us
  waiting for transfers between devices  113 us (72%)
  between operations  13.5 us (9%)
  starting transfers between devices  13 us (8%)
  matrix products  9.58 us (6%)
  local copies, waits for them, and re-layouts  5.61 us (4%)
  other arithmetic  1.79 us (1%)
    reduce_scatter x1, waiting for transfers between devices, body(): mine = lax.psum_scatter(recon, 'latent', scatter_dimension=0, tiled=True)  69.7 us
    all_gather x1, waiting for transfers between devices, body(): lax.all_gather(resid[0], 'latent', axis=0, tiled=True)  32.6 us
    ppermute x3, starting transfers between devices, shifted(): return lax.ppermute(shard, axis, pairs)  13 us
    ppermute x3, waiting for transfers between devices, shifted(): return lax.ppermute(shard, axis, pairs)  10.4 us
    cond x1, local copies, waits for them, and re-layouts, decode_add(): lax.cond(jnp.logical_and(source >= 0, source <= target), added, lambda va...  5.61 us
    dot_general x1, matrix products, added(): return value + jnp.dot(block, chosen, preferred_element_type=jnp.float32)  5.46 us
    dot_general x1, matrix products, body(): jnp.dot(lax.all_gather(resid[0], 'latent', axis=0, tiled=True), encoder,...  4.11 us
  transfers between devices with their start and end apart: 5, of which 4 were waited for; matrix products, arithmetic and copies ran while one was open for 3% of the time, Pallas kernels for 0%

commit v1 on v0

v1 whole, which is shorter than its diff:
```python
import functools

import jax
import jax.numpy as jnp
from jax import lax
from jax.experimental import pallas as pl
from jax.experimental.pallas import tpu as pltpu
from jax.sharding import PartitionSpec as P

F32 = jnp.float32
BF16 = jnp.bfloat16
LIMIT = 48 * 1024 * 1024


def swap(shard, even_mask, odd_mask):
    peers = lax.axis_size("latent")
    pairs = [(i, i ^ (odd_mask if i & 1 else even_mask)) for i in range(peers)]
    return lax.ppermute(shard, "latent", pairs)


def up(shard):
    layers = lax.axis_size("layer")
    return lax.ppermute(shard, "layer", [(i, i + 1) for i in range(layers - 1)])


def tile_of(total, most):
    tile = min(total, most)
    while total % tile:
        tile //= 2
    return tile


def encode_kernel(top_ref, low_ref, w_ref, b_ref, out_ref, acc_ref):
    k = pl.program_id(0)
    half = top_ref.shape[0]

    @pl.when(k == 0)
    def _():
        acc_ref[...] = jnp.zeros_like(acc_ref)

    acc_ref[:half] += jnp.dot(top_ref[...], w_ref[...], preferred_element_type=F32)
    acc_ref[half:] += jnp.dot(low_ref[...], w_ref[...], preferred_element_type=F32)

    @pl.when(k == pl.num_programs(0) - 1)
    def _():
        out_ref[...] = jnp.maximum(acc_ref[...] + b_ref[...], 0.0).astype(BF16)


def encode(top, low, w, b):
    half, depth = top.shape
    wide = w.shape[1]
    tk = tile_of(depth, 512)
    return pl.pallas_call(
        encode_kernel,
        grid=(depth // tk,),
        in_specs=[
            pl.BlockSpec((half, tk), lambda k: (0, k)),
            pl.BlockSpec((half, tk), lambda k: (0, k)),
            pl.BlockSpec((tk, wide), lambda k: (k, 0)),
            pl.BlockSpec((1, wide), lambda k: (0, 0)),
        ],
        out_specs=pl.BlockSpec((2 * half, wide), lambda k: (0, 0)),
        out_shape=jax.ShapeDtypeStruct((2 * half, wide), BF16),
        scratch_shapes=[pltpu.VMEM((2 * half, wide), F32)],
        compiler_params=pltpu.CompilerParams(vmem_limit_bytes=LIMIT),
        cost_estimate=pl.CostEstimate(
            flops=4 * half * depth * wide,
            bytes_accessed=2 * depth * wide + 4 * half * depth,
            transcendentals=0,
        ),
    )(top, low, w, b)


def decode_kernel(count, last, target_ref, *refs):
    lats, weights = refs[:count], refs[count : 2 * count]
    rest = refs[2 * count :]
    total = jnp.dot(lats[0][...], weights[0][0], preferred_element_type=F32)
    for lat, w in zip(lats[1:], weights[1:]):
        total += jnp.dot(lat[...], w[0], preferred_element_type=F32)
    if last:
        acc_ref, top_ref, low_ref = rest
        total += acc_ref[...]
        half = top_ref.shape[0]
        top_ref[...] = total[:half]
        low_ref[...] = total[half:].astype(BF16)
    else:
        rest[-1][...] = total


def decode(lats, first, target, weights, acc=None):
    count = len(lats)
    rows, depth = lats[0].shape
    wide = weights.shape[2]
    tn = tile_of(wide, 512)

    def at(j):
        return lambda n, t: (jnp.maximum(t[0] - (first + j), 0), 0, n)

    block = pl.BlockSpec((rows, tn), lambda n, t: (0, n))
    half = pl.BlockSpec((rows // 2, tn), lambda n, t: (0, n))
    last = acc is not None
    return pl.pallas_call(
        functools.partial(decode_kernel, count, last),
        grid_spec=pltpu.PrefetchScalarGridSpec(
            num_scalar_prefetch=1,
            grid=(wide // tn,),
            in_specs=[pl.BlockSpec((rows, depth), lambda n, t: (0, 0))] * count
            + [pl.BlockSpec((1, depth, tn), at(j)) for j in range(count)]
            + ([block] if last else []),
            out_specs=[half, half] if last else block,
        ),
        out_shape=[
            jax.ShapeDtypeStruct((rows // 2, wide), F32),
            jax.ShapeDtypeStruct((rows // 2, wide), BF16),
        ]
        if last
        else jax.ShapeDtypeStruct((rows, wide), F32),
        compiler_params=pltpu.CompilerParams(vmem_limit_bytes=LIMIT),
        cost_estimate=pl.CostEstimate(
            flops=2 * count * rows * depth * wide,
            bytes_accessed=2 * count * depth * wide + 8 * rows * wide,
            transcendentals=0,
        ),
    )(target, *lats, *([weights] * count), *([acc] if last else []))


def body(resid, mlp_out, enc_w, enc_b, dec_w):
    target = lax.axis_index("layer").reshape(1)
    layers = lax.axis_size("layer")
    peers = lax.axis_size("latent")
    weights = dec_w[0]
    masks = [1 << bit for bit in range(1, peers.bit_length() - 1)]
    steps = list(zip(masks, masks[::-1]))

    held = resid[0]
    for even, odd in steps:
        held = jnp.concatenate([held, swap(held, even, odd)], 0)
    carried = encode(held, swap(held, 1, 1), enc_w[0], enc_b)

    lats = [carried]
    for _ in range(layers - 2):
        carried = up(carried)
        lats.append(carried)
    final = up(carried)
    early = decode(lats, 0, target, weights)
    top, low = decode([final], layers - 1, target, weights, early)

    total = top + swap(low, 1, 1).astype(F32)
    for even, odd in steps[::-1]:
        half = total.shape[0] // 2
        total = total[:half] + swap(total[half:].astype(BF16), even, odd).astype(F32)
    return (mlp_out[0].astype(F32) - total).astype(BF16)[None]


def solution(mesh):
    return jax.shard_map(
        body,
        mesh=mesh,
        in_specs=(
            P("layer", "latent", None),
            P("layer", "latent", None),
            P("layer", None, "latent"),
            P("layer", "latent"),
            P("layer", None, "latent", None),
        ),
        out_specs=P("layer", "latent", None),
        check_vma=False,
    )
```

time: 157 us -> 89.8 us (0.57)
  waiting for transfers between devices: 113 us -> 40.4 us
  Pallas kernels: 0 us -> 22.3 us
  between operations: 13.5 us -> 0.13 us
  matrix products: 9.58 us -> 0 us
  starting transfers between devices: 13 us -> 21.1 us
  local copies, waits for them, and re-layouts: 5.61 us -> 2.04 us
    reduce_scatter x1 -> x0, waiting for transfers between devices: 69.7 us -> none  [body(): mine = lax.psum_scatter(recon, 'latent', scatter_dimension=0, tiled=True)]
    all_gather x1 -> x0, waiting for transfers between devices: 32.6 us -> none  [body(): lax.all_gather(resid[0], 'latent', axis=0, tiled=True)]
    ppermute x3 -> x9, waiting for transfers between devices: 10.4 us -> 40.4 us  [the longest x6 29.5 us: swap(): return lax.ppermute(shard, 'latent', pairs)]
    pallas_call x0 -> x3, Pallas kernels: none -> 22.3 us  [the longest x2 16.3 us: decode(): pl.pallas_call(functools.partial(decode_kernel, count, last), grid_spec=p...]
    dot_general x2 -> x0, matrix products: 9.58 us -> none  [the longest x1 5.46 us: added(): return value + jnp.dot(block, chosen, preferred_element_type=jnp.float32)]
    ppermute x3 -> x9, starting transfers between devices: 13 us -> 21.1 us  [the longest x3 12.8 us: up(): return lax.ppermute(shard, 'layer', [(i, i + 1) for i in range(layers - 1)])]
    cond x1 -> x0, local copies, waits for them, and re-layouts: 5.61 us -> none  [decode_add(): lax.cond(jnp.logical_and(source >= 0, source <= target), added, lambda va...]
    concatenate x0 -> x2, other arithmetic: none -> 2.02 us  [body(): held = jnp.concatenate([held, swap(held, even, odd)], 0)]
  transfers between devices with their start and end apart: 5 -> 9, of which waited for: 4 -> 8; matrix products, arithmetic and copies ran while one was open for 3% -> 0% of each run, Pallas kernels for 0% -> 11%
where the time goes in v1:
time: 89.8 us; the launch traced here: 89.2 us
  waiting for transfers between devices  40.4 us (45%)
  Pallas kernels  22.3 us (25%)
  starting transfers between devices  21.1 us (23%)
  other arithmetic  3.17 us (4%)
  local copies, waits for them, and re-layouts  2.04 us (2%)
    ppermute x6, waiting for transfers between devices, swap(): return lax.ppermute(shard, 'latent', pairs)  29.5 us
    pallas_call x2, Pallas kernels, decode(): pl.pallas_call(functools.partial(decode_kernel, count, last), grid_spec=p...  16.3 us
    ppermute x3, starting transfers between devices, up(): return lax.ppermute(shard, 'layer', [(i, i + 1) for i in range(layers - 1)])  12.8 us
    ppermute x3, waiting for transfers between devices, up(): return lax.ppermute(shard, 'layer', [(i, i + 1) for i in range(layers - 1)])  10.8 us
    ppermute x6, starting transfers between devices, swap(): return lax.ppermute(shard, 'latent', pairs)  8.36 us
    pallas_call x1, Pallas kernels, encode(): pl.pallas_call(encode_kernel, grid=(depth // tk,), in_specs=[pl.BlockSpec...  6.06 us
    concatenate x2, other arithmetic, body(): held = jnp.concatenate([held, swap(held, even, odd)], 0)  2.02 us
    unnamed x6, local copies, waits for them, and re-layouts  1.95 us
  transfers between devices with their start and end apart: 9, of which 8 were waited for; matrix products, arithmetic and copies ran while one was open for 0% of the time, Pallas kernels for 11%

profile of v1, /device:TPU:0, one launch (start us, length us, event | category | flops | bytes accessed | tf_op | source)
XLA Modules:
  0.0 89.2 jit_solution(1083008790072609269)
XLA Ops:
  0.0 2.9 %collective-permute-start = (bf16[32,4096]{1,0:T(8,128)(2,1)}, bf16[32,4096]{1,0:T(8,128)(2,1)S(1)}, u32[]{:S(2)}, u32[]{:S(2)}) collective-permute-start(bf16[32,4096]{1,0:T(8,128)(2,1)} %bitcast.14), channel_id=1, source_target_pairs={{0,2},{1,5},{2,0},{3,7},{4,6},{5,1},{6,4},{7,3},{8,10},{9,13},{10,... | collective-permute-start | bytes 786440 | tf_op jit(solution)/shard_map/ppermute | solution.py:18
  2.9 4.6 %collective-permute-done = bf16[32,4096]{1,0:T(8,128)(2,1)S(1)} collective-permute-done((bf16[32,4096]{1,0:T(8,128)(2,1)}, bf16[32,4096]{1,0:T(8,128)(2,1)S(1)}, u32[]{:S(2)}, u32[]{:S(2)}) %collective-permute-start) | collective-permute-done | bytes 262176 | tf_op jit(solution)/shard_map/ppermute | solution.py:18
  7.5 1.0 %pad_maximum_fusion.1 = bf16[64,4096]{1,0:T(8,128)(2,1)S(1)} fusion(bf16[32,4096]{1,0:T(8,128)(2,1)S(1)} %collective-permute-done, bf16[32,4096]{1,0:T(8,128)(2,1)} %bitcast.15), kind=kLoop, calls=%fused_computation.8 | loop fusion | flops 1048576 | bytes 1048576 | tf_op jit(solution)/shard_map/concatenate | solution.py:137
  8.5 2.1 %collective-permute-start.1 = (bf16[64,4096]{1,0:T(8,128)(2,1)S(1)}, bf16[64,4096]{1,0:T(8,128)(2,1)S(1)}, u32[]{:S(2)}, u32[]{:S(2)}) collective-permute-start(bf16[64,4096]{1,0:T(8,128)(2,1)S(1)} %pad_maximum_fusion.1), channel_id=1, source_target_pairs={{0,4},{1,3},{2,6},{3,1},{4,0},{5,7},{6,2},{7,5},{8,12},{9,11},{10,... | collective-permute-start | bytes 1572872 | tf_op jit(solution)/shard_map/ppermute | solution.py:18
  10.6 7.2 %collective-permute-done.1 = bf16[64,4096]{1,0:T(8,128)(2,1)S(1)} collective-permute-done((bf16[64,4096]{1,0:T(8,128)(2,1)S(1)}, bf16[64,4096]{1,0:T(8,128)(2,1)S(1)}, u32[]{:S(2)}, u32[]{:S(2)}) %collective-permute-start.1) | collective-permute-done | bytes 524320 | tf_op jit(solution)/shard_map/ppermute | solution.py:18
  17.8 1.0 %pad_maximum_fusion.top_ref = bf16[128,4096]{1,0:T(8,128)(2,1)S(1)} fusion(bf16[64,4096]{1,0:T(8,128)(2,1)S(1)} %collective-permute-done.1, bf16[32,4096]{1,0:T(8,128)(2,1)S(1)} %collective-permute-done, bf16[32,4096]{1,0:T(8,128)(2,1)} %bitcast.16), kind=kLoop, calls=%fused_computation.3 | loop fusion | flops 3145728 | bytes 2097152 | tf_op jit(solution)/shard_map/concatenate | solution.py:137
  18.8 0.1 collective-permute-start.2
  18.9 2.6 %collective-permute-done.2.low_ref = bf16[128,4096]{1,0:T(8,128)(2,1)S(1)} collective-permute-done((bf16[128,4096]{1,0:T(8,128)(2,1)S(1)}, bf16[128,4096]{1,0:T(8,128)(2,1)S(1)}, u32[]{:S(2)}, u32[]{:S(2)}) %collective-permute-start.2) | collective-permute-done | bytes 1048608 | tf_op jit(solution)/shard_map/ppermute | solution.py:18
  21.5 0.0 copy-done.1
  21.5 6.1 %shard_map.55.refs_0_ = bf16[256,512]{1,0:T(8,128)(2,1)S(1)} custom-call(bf16[128,4096]{1,0:T(8,128)(2,1)S(1)} %pad_maximum_fusion.top_ref, bf16[128,4096]{1,0:T(8,128)(2,1)S(1)} %collective-permute-done.2.low_ref, bf16[4096,512]{1,0:T(8,128)(2,1)} %bitcast.13, f32[1,512]{1,0:T(1,128)S(1)} %copy-done.1), custom_call_target="tpu_custom_call" | custom-call | flops 1073741824 | bytes 6291456 | tf_op jit(solution)/shard_map/pallas_call | solution.py:53
  27.6 4.0 %collective-permute-start.3 = (bf16[256,512]{1,0:T(8,128)(2,1)S(1)}, bf16[256,512]{1,0:T(8,128)(2,1)S(1)}, u32[]{:S(2)}, u32[]{:S(2)}) collective-permute-start(bf16[256,512]{1,0:T(8,128)(2,1)S(1)} %shard_map.55.refs_0_), channel_id=1, source_target_pairs={{0,8},{8,16},{16,24},{1,9},{9,17},{17,25},{2,10},{10,18},{18,26},{... | collective-permute-start | bytes 786440 | tf_op jit(solution)/shard_map/ppermute | solution.py:23
  31.6 5.8 %collective-permute-done.3.refs_1_ = bf16[256,512]{1,0:T(8,128)(2,1)S(1)} collective-permute-done((bf16[256,512]{1,0:T(8,128)(2,1)S(1)}, bf16[256,512]{1,0:T(8,128)(2,1)S(1)}, u32[]{:S(2)}, u32[]{:S(2)}) %collective-permute-start.3) | collective-permute-done | bytes 262176 | tf_op jit(solution)/shard_map/ppermute | solution.py:23
  37.4 4.4 %collective-permute-start.4 = (bf16[256,512]{1,0:T(8,128)(2,1)S(1)}, bf16[256,512]{1,0:T(8,128)(2,1)S(1)}, u32[]{:S(2)}, u32[]{:S(2)}) collective-permute-start(bf16[256,512]{1,0:T(8,128)(2,1)S(1)} %collective-permute-done.3.refs_1_), channel_id=1, source_target_pairs={{0,8},{8,16},{16,24},{1,9},{9,17},{17,25},{2,10},{10,18},{18,26},{... | collective-permute-start | bytes 786440 | tf_op jit(solution)/shard_map/ppermute | solution.py:23
  41.8 5.0 %collective-permute-done.4.refs_2_ = bf16[256,512]{1,0:T(8,128)(2,1)S(1)} collective-permute-done((bf16[256,512]{1,0:T(8,128)(2,1)S(1)}, bf16[256,512]{1,0:T(8,128)(2,1)S(1)}, u32[]{:S(2)}, u32[]{:S(2)}) %collective-permute-start.4) | collective-permute-done | bytes 262176 | tf_op jit(solution)/shard_map/ppermute | solution.py:23
  46.8 4.4 %collective-permute-start.5 = (bf16[256,512]{1,0:T(8,128)(2,1)S(1)}, bf16[256,512]{1,0:T(8,128)(2,1)S(1)}, u32[]{:S(2)}, u32[]{:S(2)}) collective-permute-start(bf16[256,512]{1,0:T(8,128)(2,1)S(1)} %collective-permute-done.4.refs_2_), channel_id=1, source_target_pairs={{0,8},{8,16},{16,24},{1,9},{9,17},{17,25},{2,10},{10,18},{18,26},{... | collective-permute-start | bytes 786440 | tf_op jit(solution)/shard_map/ppermute | solution.py:23
  51.2 9.5 %shard_map.56.refs_2_ = f32[256,4096]{1,0:T(8,128)S(1)} custom-call(s32[1]{0:T(128)} %bitcast.1.target_ref, bf16[256,512]{1,0:T(8,128)(2,1)S(1)} %shard_map.55.refs_0_, bf16[256,512]{1,0:T(8,128)(2,1)S(1)} %collective-permute-done.3.refs_1_, bf16[256,512]{1,0:T(8,128)(2,1)S(1)} %collective-permute-done.4.refs_2_, bf16[4,512,4096]{2,1,0:T(8,128)(2,1)} %bitcast.9, ...), custom_call_target="tpu_custom_call" | custom-call | flops 3221225472 | bytes 20971520 | tf_op jit(solution)/shard_map/pallas_call | solution.py:102
  60.8 0.0 copy-start
  60.8 1.9 %copy-done = f32[256,4096]{1,0:T(8,128)} copy-done((f32[256,4096]{1,0:T(8,128)}, f32[256,4096]{1,0:T(8,128)S(1)}, u32[]{:S(2)}) %copy-start) | copy-done | bytes 4194328
  62.7 0.0 collective-permute-done.5.refs_0_
  62.7 6.7 %shard_map.57 = (f32[128,4096]{1,0:T(8,128)S(1)}, bf16[128,4096]{1,0:T(8,128)(2,1)S(1)}) custom-call(s32[1]{0:T(128)} %bitcast.1.target_ref, bf16[256,512]{1,0:T(8,128)(2,1)S(1)} %collective-permute-done.5.refs_0_, bf16[4,512,4096]{2,1,0:T(8,128)(2,1)} %bitcast.12, f32[256,4096]{1,0:T(8,128)} %copy-done), custom_call_target="tpu_custom_call" | custom-call | flops 1073741824 | bytes 12582912 | tf_op jit(solution)/shard_map/pallas_call | solution.py:102
  69.5 0.1 collective-permute-start.6
  69.6 2.6 %collective-permute-done.6 = bf16[128,4096]{1,0:T(8,128)(2,1)S(1)} collective-permute-done((bf16[128,4096]{1,0:T(8,128)(2,1)S(1)}, bf16[128,4096]{1,0:T(8,128)(2,1)S(1)}, u32[]{:S(2)}, u32[]{:S(2)}) %collective-permute-start.6) | collective-permute-done | bytes 1048608 | tf_op jit(solution)/shard_map/ppermute | solution.py:18
  72.2 0.2 convert_add_fusion
  72.5 0.0 copy-start.2
  72.5 0.1 slice.32
  72.5 1.6 %collective-permute-start.7 = (bf16[64,4096]{1,0:T(8,128)(2,1)S(1)}, bf16[64,4096]{1,0:T(8,128)(2,1)S(1)}, u32[]{:S(2)}, u32[]{:S(2)}) collective-permute-start(bf16[64,4096]{1,0:T(8,128)(2,1)S(1)} %slice.32), channel_id=1, source_target_pairs={{0,4},{1,3},{2,6},{3,1},{4,0},{5,7},{6,2},{7,5},{8,12},{9,11},{10,... | collective-permute-start | bytes 1572872 | tf_op jit(solution)/shard_map/ppermute | solution.py:18
  74.1 7.6 %collective-permute-done.7 = bf16[64,4096]{1,0:T(8,128)(2,1)S(1)} collective-permute-done((bf16[64,4096]{1,0:T(8,128)(2,1)S(1)}, bf16[64,4096]{1,0:T(8,128)(2,1)S(1)}, u32[]{:S(2)}, u32[]{:S(2)}) %collective-permute-start.7) | collective-permute-done | bytes 524320 | tf_op jit(solution)/shard_map/ppermute | solution.py:18
  81.8 0.1 slice_add_fusion
  82.0 1.6 %collective-permute-start.8 = (bf16[32,4096]{1,0:T(8,128)(2,1)S(1)}, bf16[32,4096]{1,0:T(8,128)(2,1)S(1)}, u32[]{:S(2)}, u32[]{:S(2)}) collective-permute-start(bf16[32,4096]{1,0:T(8,128)(2,1)S(1)} %slice.33), channel_id=1, source_target_pairs={{0,2},{1,5},{2,0},{3,7},{4,6},{5,1},{6,4},{7,3},{8,10},{9,13},{10,... | collective-permute-start | bytes 786440 | tf_op jit(solution)/shard_map/ppermute | solution.py:18
  83.5 4.9 %collective-permute-done.8 = bf16[32,4096]{1,0:T(8,128)(2,1)S(1)} collective-permute-done((bf16[32,4096]{1,0:T(8,128)(2,1)S(1)}, bf16[32,4096]{1,0:T(8,128)(2,1)S(1)}, u32[]{:S(2)}, u32[]{:S(2)}) %collective-permute-start.8) | collective-permute-done | bytes 262176 | tf_op jit(solution)/shard_map/ppermute | solution.py:18
  88.4 0.0 copy-done.2
  88.4 0.8 fusion.2
  (2 shorter events, 0.0 us)
Async XLA Ops:
  0.0 21.5 %copy-start.1 = (f32[1,512]{1,0:T(1,128)S(1)}, f32[1,512]{1,0:T(1,128)}, u32[]{:S(2)}) copy-start(f32[1,512]{1,0:T(1,128)} %b_ref.1) | copy-start | bytes 6148
  0.0 7.5 %collective-permute-start = (bf16[32,4096]{1,0:T(8,128)(2,1)}, bf16[32,4096]{1,0:T(8,128)(2,1)S(1)}, u32[]{:S(2)}, u32[]{:S(2)}) collective-permute-start(bf16[32,4096]{1,0:T(8,128)(2,1)} %bitcast.14), channel_id=1, source_target_pairs={{0,2},{1,5},{2,0},{3,7},{4,6},{5,1},{6,4},{7,3},{8,10},{9,13},{10,... | collective-permute-start | bytes 786440 | tf_op jit(solution)/shard_map/ppermute | solution.py:18
  8.5 9.3 %collective-permute-start.1 = (bf16[64,4096]{1,0:T(8,128)(2,1)S(1)}, bf16[64,4096]{1,0:T(8,128)(2,1)S(1)}, u32[]{:S(2)}, u32[]{:S(2)}) collective-permute-start(bf16[64,4096]{1,0:T(8,128)(2,1)S(1)} %pad_maximum_fusion.1), channel_id=1, source_target_pairs={{0,4},{1,3},{2,6},{3,1},{4,0},{5,7},{6,2},{7,5},{8,12},{9,11},{10,... | collective-permute-start | bytes 1572872 | tf_op jit(solution)/shard_map/ppermute | solution.py:18
  18.8 2.7 %collective-permute-start.2 = (bf16[128,4096]{1,0:T(8,128)(2,1)S(1)}, bf16[128,4096]{1,0:T(8,128)(2,1)S(1)}, u32[]{:S(2)}, u32[]{:S(2)}) collective-permute-start(bf16[128,4096]{1,0:T(8,128)(2,1)S(1)} %pad_maximum_fusion.top_ref), channel_id=1, source_target_pairs={{0,1},{1,0},{2,3},{3,2},{4,5},{5,4},{6,7},{7,6},{8,9},{9,8},{10,11... | collective-permute-start | bytes 3145736 | tf_op jit(solution)/shard_map/ppermute | solution.py:18
  27.6 9.8 %collective-permute-start.3 = (bf16[256,512]{1,0:T(8,128)(2,1)S(1)}, bf16[256,512]{1,0:T(8,128)(2,1)S(1)}, u32[]{:S(2)}, u32[]{:S(2)}) collective-permute-start(bf16[256,512]{1,0:T(8,128)(2,1)S(1)} %shard_map.55.refs_0_), channel_id=1, source_target_pairs={{0,8},{8,16},{16,24},{1,9},{9,17},{17,25},{2,10},{10,18},{18,26},{... | collective-permute-start | bytes 786440 | tf_op jit(solution)/shard_map/ppermute | solution.py:23
  37.4 9.4 %collective-permute-start.4 = (bf16[256,512]{1,0:T(8,128)(2,1)S(1)}, bf16[256,512]{1,0:T(8,128)(2,1)S(1)}, u32[]{:S(2)}, u32[]{:S(2)}) collective-permute-start(bf16[256,512]{1,0:T(8,128)(2,1)S(1)} %collective-permute-done.3.refs_1_), channel_id=1, source_target_pairs={{0,8},{8,16},{16,24},{1,9},{9,17},{17,25},{2,10},{10,18},{18,26},{... | collective-permute-start | bytes 786440 | tf_op jit(solution)/shard_map/ppermute | solution.py:23
  46.8 15.9 %collective-permute-start.5 = (bf16[256,512]{1,0:T(8,128)(2,1)S(1)}, bf16[256,512]{1,0:T(8,128)(2,1)S(1)}, u32[]{:S(2)}, u32[]{:S(2)}) collective-permute-start(bf16[256,512]{1,0:T(8,128)(2,1)S(1)} %collective-permute-done.4.refs_2_), channel_id=1, source_target_pairs={{0,8},{8,16},{16,24},{1,9},{9,17},{17,25},{2,10},{10,18},{18,26},{... | collective-permute-start | bytes 786440 | tf_op jit(solution)/shard_map/ppermute | solution.py:23
  60.8 2.0 %copy-start = (f32[256,4096]{1,0:T(8,128)}, f32[256,4096]{1,0:T(8,128)S(1)}, u32[]{:S(2)}) copy-start(f32[256,4096]{1,0:T(8,128)S(1)} %shard_map.56.refs_2_) | copy-start | bytes 12582916
  69.5 2.7 %collective-permute-start.6 = (bf16[128,4096]{1,0:T(8,128)(2,1)S(1)}, bf16[128,4096]{1,0:T(8,128)(2,1)S(1)}, u32[]{:S(2)}, u32[]{:S(2)}) collective-permute-start(bf16[128,4096]{1,0:T(8,128)(2,1)S(1)} %get-tuple-element.8), channel_id=1, source_target_pairs={{0,1},{1,0},{2,3},{3,2},{4,5},{5,4},{6,7},{7,6},{8,9},{9,8},{10,11... | collective-permute-start | bytes 3145736 | tf_op jit(solution)/shard_map/ppermute | solution.py:18
  72.5 15.9 %copy-start.2 = (bf16[1,32,4096]{2,1,0:T(8,128)(2,1)S(1)}, bf16[1,32,4096]{2,1,0:T(8,128)(2,1)}, u32[]{:S(2)}) copy-start(bf16[1,32,4096]{2,1,0:T(8,128)(2,1)} %param.6) | copy-start | bytes 786436
  72.5 9.2 %collective-permute-start.7 = (bf16[64,4096]{1,0:T(8,128)(2,1)S(1)}, bf16[64,4096]{1,0:T(8,128)(2,1)S(1)}, u32[]{:S(2)}, u32[]{:S(2)}) collective-permute-start(bf16[64,4096]{1,0:T(8,128)(2,1)S(1)} %slice.32), channel_id=1, source_target_pairs={{0,4},{1,3},{2,6},{3,1},{4,0},{5,7},{6,2},{7,5},{8,12},{9,11},{10,... | collective-permute-start | bytes 1572872 | tf_op jit(solution)/shard_map/ppermute | solution.py:18
  82.0 6.4 %collective-permute-start.8 = (bf16[32,4096]{1,0:T(8,128)(2,1)S(1)}, bf16[32,4096]{1,0:T(8,128)(2,1)S(1)}, u32[]{:S(2)}, u32[]{:S(2)}) collective-permute-start(bf16[32,4096]{1,0:T(8,128)(2,1)S(1)} %slice.33), channel_id=1, source_target_pairs={{0,2},{1,5},{2,0},{3,7},{4,6},{5,1},{6,4},{7,3},{8,10},{9,13},{10,... | collective-permute-start | bytes 786440 | tf_op jit(solution)/shard_map/ppermute | solution.py:18

commit v2 on v0

v2 whole, which is shorter than its diff:
```python
import functools

import jax
import jax.numpy as jnp
from jax import lax
from jax.experimental import pallas as pl
from jax.experimental.pallas import tpu as pltpu
from jax.sharding import PartitionSpec as P

F32 = jnp.float32
BF16 = jnp.bfloat16
MIB = 1024 * 1024
WHOLE = pl.BlockSpec(memory_space=pltpu.VMEM)
FAR = pl.BlockSpec(memory_space=pltpu.HBM)
SCALAR = pl.BlockSpec(memory_space=pltpu.SMEM)


def swap(shard, masks):
    peers = lax.axis_size("latent")
    return lax.ppermute(shard, "latent", [(i, i ^ masks[i & 1]) for i in range(peers)])


def up(shard, by, back):
    layers = lax.axis_size("layer")
    return lax.ppermute(shard, "layer", [(i - by, i) for i in range(back, layers)])


def after(value, *others):
    return lax.optimization_barrier((value, *others))[0]


def tile_of(total, most):
    tile = min(total, most)
    while total % tile:
        tile //= 2
    return tile


def run_all(copies):
    for copy in copies:
        copy.start()
    for copy in copies:
        copy.wait()


def load_kernel(count, cuts, *refs):
    srcs, dsts, sems = refs[:count], refs[count : 2 * count], refs[2 * count]
    copies = []
    for n, (src, dst, cut) in enumerate(zip(srcs, dsts, cuts)):
        rows = src.shape[0] // cut
        for i in range(cut):
            part = pl.ds(i * rows, rows)
            copies.append(pltpu.make_async_copy(src.at[part], dst.at[part], sems.at[sum(cuts[:n]) + i]))
    run_all(copies)


def load(arrays, cuts):
    count = len(arrays)
    return pl.pallas_call(
        functools.partial(load_kernel, count, cuts),
        in_specs=[FAR] * count,
        out_specs=[WHOLE] * count,
        out_shape=[pltpu.VMEM(a.shape, a.dtype) for a in arrays],
        scratch_shapes=[pltpu.SemaphoreType.DMA((sum(cuts),))],
        compiler_params=pltpu.CompilerParams(vmem_limit_bytes=2 * MIB),
        cost_estimate=pl.CostEstimate(flops=1024, bytes_accessed=1024, transcendentals=0),
    )(*[pltpu.with_memory_space_constraint(a, pltpu.HBM) for a in arrays])


def pick_kernel(cuts, target_ref, src_ref, *refs):
    dsts, sems = refs[:-1], refs[-1]
    rows = dsts[0].shape[0] // cuts
    copies = []
    for back, dst_ref in enumerate(dsts):
        source = jnp.maximum(target_ref[0] - back, 0)
        for i in range(cuts):
            part = pl.ds(i * rows, rows)
            copies.append(pltpu.make_async_copy(src_ref.at[source, part], dst_ref.at[part], sems.at[back, i]))
    run_all(copies)


def pick(weights, target):
    count, depth, wide = weights.shape
    cuts = 2
    return pl.pallas_call(
        functools.partial(pick_kernel, cuts),
        in_specs=[SCALAR, FAR],
        out_specs=[WHOLE] * count,
        out_shape=[pltpu.VMEM((depth, wide), weights.dtype)] * count,
        scratch_shapes=[pltpu.SemaphoreType.DMA((count, cuts))],
        compiler_params=pltpu.CompilerParams(vmem_limit_bytes=2 * MIB),
        cost_estimate=pl.CostEstimate(flops=1024, bytes_accessed=1024, transcendentals=0),
    )(target, pltpu.with_memory_space_constraint(weights, pltpu.HBM))


def encode_kernel(count, *refs):
    pieces, (w_ref, b_ref, out_ref) = refs[:count], refs[count:]
    rows = jnp.concatenate([piece[...] for piece in pieces], 0)
    pre = jnp.dot(rows, w_ref[...], preferred_element_type=F32) + b_ref[...]
    out_ref[...] = jnp.maximum(pre, 0.0).astype(BF16)


def encode(pieces, w, b):
    count = len(pieces)
    rows = sum(piece.shape[0] for piece in pieces)
    depth, wide = w.shape
    return pl.pallas_call(
        functools.partial(encode_kernel, count),
        in_specs=[WHOLE] * (count + 2),
        out_specs=WHOLE,
        out_shape=pltpu.VMEM((rows, wide), BF16),
        compiler_params=pltpu.CompilerParams(vmem_limit_bytes=16 * MIB),
        cost_estimate=pl.CostEstimate(flops=1024, bytes_accessed=1024, transcendentals=0),
    )(*pieces, w, b)


def decode_kernel(count, tile, summed, halved, *refs):
    lats, ws, rest = refs[:count], refs[count : 2 * count], refs[2 * count :]
    wide = ws[0].shape[1]

    @pl.loop(0, wide // tile)
    def _(n):
        columns = pl.ds(pl.multiple_of(n * tile, tile), tile)
        total = jnp.dot(lats[0][...], ws[0][:, columns], preferred_element_type=F32)
        for lat, w in zip(lats[1:], ws[1:]):
            total += jnp.dot(lat[...], w[:, columns], preferred_element_type=F32)
        if summed:
            total += rest[0][:, columns]
        if halved:
            top_ref, low_ref = rest[-2:]
            half = top_ref.shape[0]
            top_ref[:, columns] = total[:half]
            low_ref[:, columns] = total[half:].astype(BF16)
        else:
            rest[-1][:, columns] = total


def decode(lats, weights, acc=None, halved=False):
    count = len(lats)
    rows, depth = lats[0].shape
    wide = weights[0].shape[1]
    summed = acc is not None
    halves = [pltpu.VMEM((rows // 2, wide), F32), pltpu.VMEM((rows // 2, wide), BF16)]
    return pl.pallas_call(
        functools.partial(decode_kernel, count, tile_of(wide, 2048), summed, halved),
        in_specs=[WHOLE] * (2 * count + summed),
        out_specs=[WHOLE, WHOLE] if halved else WHOLE,
        out_shape=halves if halved else pltpu.VMEM((rows, wide), F32),
        compiler_params=pltpu.CompilerParams(vmem_limit_bytes=8 * MIB),
        cost_estimate=pl.CostEstimate(flops=1024, bytes_accessed=1024, transcendentals=0),
    )(*lats, *weights, *([acc] if summed else []))


def body(resid, mlp_out, enc_w, enc_b, dec_w):
    target = lax.axis_index("layer").reshape(1)
    layers = lax.axis_size("layer")
    peers = lax.axis_size("latent")
    bits = [1 << bit for bit in range(1, peers.bit_length() - 1)]
    steps = list(zip(bits, bits[::-1]))

    pieces = [resid[0]]
    for masks in steps:
        pieces += [swap(piece, masks) for piece in pieces]
    count = len(pieces)
    half = count // 2
    encoder, bias, mine = load([after(enc_w[0], pieces[half]), enc_b, resid[0]], [4, 1, 1])
    pieces[-1] = after(pieces[-1], encoder)
    mates = [swap(piece, (1, 1)) for piece in pieces]
    pieces[0] = mine

    def gather(group, *gate):
        return encode([after(pieces[i], *gate) for i in group] + [mates[i] for i in group], encoder, bias)

    def lift(held, *gate):
        for j in range(len(held), layers):
            held.append(up(after(held[j - 1], *gate) if j > 2 else held[j - 1], 1, j) if j % 2 else up(held[j - 2], 2, j))

    far = [gather(range(half, count))]
    near = [gather(range(half), far[0])]
    weights = pick(after(dec_w[0], near[0]), target)
    lift(far, weights[0])
    lift(near, weights[0])
    sums = [decode([after(lat, near[2]) for lat in held[:-1]], weights[:-1]) for held in (far, near)]
    top, low = decode([after(far[-1], near[-1], sums[1])], weights[-1:], sums[0], True)
    ends = [top + swap(low, (1, 1)).astype(F32)]
    top, low = decode([after(near[-1], low)], weights[-1:], sums[1], True)
    ends.insert(0, top + swap(low, (1, 1)).astype(F32))
    each = resid.shape[1]
    totals = [end[i * each : (i + 1) * each] for end in ends for i in range(half)]
    for masks in steps[::-1]:
        half = len(totals) // 2
        for i in reversed(range(half)):
            totals[i] = totals[i] + swap(totals[half + i].astype(BF16), masks).astype(F32)
        totals = totals[:half]
    return (mlp_out[0].astype(F32) - totals[0]).astype(BF16)[None]


def solution(mesh):
    return jax.shard_map(
        body,
        mesh=mesh,
        in_specs=(
            P("layer", "latent", None),
            P("layer", "latent", None),
            P("layer", None, "latent"),
            P("layer", "latent"),
            P("layer", None, "latent", None),
        ),
        out_specs=P("layer", "latent", None),
        check_vma=False,
    )
```

time: 157 us -> 60.1 us (0.38)
  waiting for transfers between devices: 113 us -> 18.6 us
  Pallas kernels: 0 us -> 15.9 us
  between operations: 13.5 us -> 0.23 us
  starting transfers between devices: 13 us -> 24.1 us
  matrix products: 9.58 us -> 0 us
  local copies, waits for them, and re-layouts: 5.61 us -> 0.05 us
    reduce_scatter x1 -> x0, waiting for transfers between devices: 69.7 us -> none  [body(): mine = lax.psum_scatter(recon, 'latent', scatter_dimension=0, tiled=True)]
    all_gather x1 -> x0, waiting for transfers between devices: 32.6 us -> none  [body(): lax.all_gather(resid[0], 'latent', axis=0, tiled=True)]
    pallas_call x0 -> x8, Pallas kernels: none -> 15.9 us  [the longest x1 6.26 us: pick(): pl.pallas_call(functools.partial(pick_kernel, cuts), in_specs=[SCALAR, FA...]
    ppermute x3 -> x18, starting transfers between devices: 13 us -> 24.1 us  [the longest x6 13.4 us: up(): lax.ppermute(shard, 'layer', [(i - by, i) for i in range(back, layers)])]
    dot_general x2 -> x0, matrix products: 9.58 us -> none  [the longest x1 5.46 us: added(): return value + jnp.dot(block, chosen, preferred_element_type=jnp.float32)]
    ppermute x3 -> x18, waiting for transfers between devices: 10.4 us -> 18.6 us  [the longest x12 18.6 us: swap(): lax.ppermute(shard, 'latent', [(i, i ^ masks[i & 1]) for i in range(peers)])]
    cond x1 -> x0, local copies, waits for them, and re-layouts: 5.61 us -> none  [decode_add(): lax.cond(jnp.logical_and(source >= 0, source <= target), added, lambda va...]
  transfers between devices with their start and end apart: 5 -> 18, of which waited for: 4 -> 7; matrix products, arithmetic and copies ran while one was open for 3% -> 0% of each run, Pallas kernels for 0% -> 25%
where the time goes in v2:
time: 60.1 us; the launch traced here: 59.9 us
  starting transfers between devices  24.1 us (40%)
  waiting for transfers between devices  18.6 us (31%)
  Pallas kernels  15.9 us (26%)
  other arithmetic  1.04 us (2%)
    ppermute x12, waiting for transfers between devices, swap(): lax.ppermute(shard, 'latent', [(i, i ^ masks[i & 1]) for i in range(peers)])  18.6 us
    ppermute x6, starting transfers between devices, up(): lax.ppermute(shard, 'layer', [(i - by, i) for i in range(back, layers)])  13.4 us
    ppermute x12, starting transfers between devices, swap(): lax.ppermute(shard, 'latent', [(i, i ^ masks[i & 1]) for i in range(peers)])  10.7 us
    pallas_call x1, Pallas kernels, pick(): pl.pallas_call(functools.partial(pick_kernel, cuts), in_specs=[SCALAR, FA...  6.26 us
    pallas_call x4, Pallas kernels, decode(): pl.pallas_call(functools.partial(decode_kernel, count, tile_of(wide, 2048...  5.8 us
    pallas_call x1, Pallas kernels, load(): pl.pallas_call(functools.partial(load_kernel, count, cuts), in_specs=[FAR...  2.28 us
    pallas_call x2, Pallas kernels, encode(): pl.pallas_call(functools.partial(encode_kernel, count), in_specs=[WHOLE]...  1.52 us
  transfers between devices with their start and end apart: 18, of which 7 were waited for; matrix products, arithmetic and copies ran while one was open for 0% of the time, Pallas kernels for 25%

profile of v2, /device:TPU:0, one launch (start us, length us, event | category | flops | bytes accessed | tf_op | source)
XLA Modules:
  0.0 59.9 jit_solution(16479398334915875645)
XLA Ops:
  0.0 2.9 %collective-permute-start.1 = (bf16[32,4096]{1,0:T(8,128)(2,1)}, bf16[32,4096]{1,0:T(8,128)(2,1)S(1)}, u32[]{:S(2)}, u32[]{:S(2)}) collective-permute-start(bf16[32,4096]{1,0:T(8,128)(2,1)} %bitcast.11), channel_id=1, source_target_pairs={{0,2},{1,5},{2,0},{3,7},{4,6},{5,1},{6,4},{7,3},{8,10},{9,13},{10,... | collective-permute-start | bytes 786440 | tf_op jit(solution)/shard_map/ppermute | solution.py:20
  2.9 1.5 %collective-permute-start = (bf16[32,4096]{1,0:T(8,128)(2,1)}, bf16[32,4096]{1,0:T(8,128)(2,1)S(1)}, u32[]{:S(2)}, u32[]{:S(2)}) collective-permute-start(bf16[32,4096]{1,0:T(8,128)(2,1)} %bitcast.12), channel_id=1, source_target_pairs={{0,4},{1,3},{2,6},{3,1},{4,0},{5,7},{6,2},{7,5},{8,12},{9,11},{10,... | collective-permute-start | bytes 786440 | tf_op jit(solution)/shard_map/ppermute | solution.py:20
  4.5 5.4 %collective-permute-done.1.refs_1_ = bf16[32,4096]{1,0:T(8,128)(2,1)S(1)} collective-permute-done((bf16[32,4096]{1,0:T(8,128)(2,1)}, bf16[32,4096]{1,0:T(8,128)(2,1)S(1)}, u32[]{:S(2)}, u32[]{:S(2)}) %collective-permute-start.1) | collective-permute-done | bytes 262176 | tf_op jit(solution)/shard_map/ppermute | solution.py:20
  9.9 1.4 %collective-permute-start.2 = (bf16[32,4096]{1,0:T(8,128)(2,1)S(1)}, bf16[32,4096]{1,0:T(8,128)(2,1)S(1)}, u32[]{:S(2)}, u32[]{:S(2)}) collective-permute-start(bf16[32,4096]{1,0:T(8,128)(2,1)S(1)} %collective-permute-done.1.refs_1_), channel_id=1, source_target_pairs={{0,4},{1,3},{2,6},{3,1},{4,0},{5,7},{6,2},{7,5},{8,12},{9,11},{10,... | collective-permute-start | bytes 786440 | tf_op jit(solution)/shard_map/ppermute | solution.py:20
  11.3 2.3 %shard_map.55 = (bf16[4096,512]{1,0:T(8,128)(2,1)S(1)}, f32[1,512]{1,0:T(1,128)S(1)}, bf16[32,4096]{1,0:T(8,128)(2,1)S(1)}) custom-call(bf16[4096,512]{1,0:T(8,128)(2,1)} %bitcast.10, f32[1,512]{1,0:T(1,128)} %refs_1_.1, bf16[32,4096]{1,0:T(8,128)(2,1)} %bitcast.13), custom_call_target="tpu_custom_call" | custom-call | flops 1024 | bytes 1024 | tf_op jit(solution)/shard_map/pallas_call | solution.py:59
  13.7 2.6 %collective-permute-done.2.refs_1_ = bf16[32,4096]{1,0:T(8,128)(2,1)S(1)} collective-permute-done((bf16[32,4096]{1,0:T(8,128)(2,1)S(1)}, bf16[32,4096]{1,0:T(8,128)(2,1)S(1)}, u32[]{:S(2)}, u32[]{:S(2)}) %collective-permute-start.2) | collective-permute-done | bytes 262176 | tf_op jit(solution)/shard_map/ppermute | solution.py:20
  16.2 0.5 collective-permute-start.5
  16.8 1.0 %collective-permute-done.4.refs_3_ = bf16[32,4096]{1,0:T(8,128)(2,1)S(1)} collective-permute-done((bf16[32,4096]{1,0:T(8,128)(2,1)S(1)}, bf16[32,4096]{1,0:T(8,128)(2,1)S(1)}, u32[]{:S(2)}, u32[]{:S(2)}) %collective-permute-start.4) | collective-permute-done | bytes 262176 | tf_op jit(solution)/shard_map/ppermute | solution.py:20
  17.8 0.7 %shard_map.56.refs_0_ = bf16[128,512]{1,0:T(8,128)(2,1)S(1)} custom-call(bf16[32,4096]{1,0:T(8,128)(2,1)S(1)} %collective-permute-done.refs_0_, bf16[32,4096]{1,0:T(8,128)(2,1)S(1)} %collective-permute-done.2.refs_1_, bf16[32,4096]{1,0:T(8,128)(2,1)S(1)} %collective-permute-done.3.refs_2_, bf16[32,4096]{1,0:T(8,128)(2,1)S(1)} %collective-permute-done.4.refs_3_, ...), custom_call_target="tpu_custom_call" | custom-call | flops 1024 | bytes 1024 | tf_op jit(solution)/shard_map/pallas_call | solution.py:107
  18.5 5.4 %collective-permute-start.9 = (bf16[128,512]{1,0:T(8,128)(2,1)S(1)}, bf16[128,512]{1,0:T(8,128)(2,1)S(1)}, u32[]{:S(2)}, u32[]{:S(2)}) collective-permute-start(bf16[128,512]{1,0:T(8,128)(2,1)S(1)} %shard_map.56.refs_0_), channel_id=1, source_target_pairs={{0,16},{8,24},{1,17},{9,25},{2,18},{10,26},{3,19},{11,27},{4,20},{... | collective-permute-start | bytes 393224 | tf_op jit(solution)/shard_map/ppermute | solution.py:25
  23.9 0.8 %shard_map.57.refs_0_ = bf16[128,512]{1,0:T(8,128)(2,1)S(1)} custom-call(bf16[32,4096]{1,0:T(8,128)(2,1)S(1)} %get-tuple-element.36.refs_0_, bf16[32,4096]{1,0:T(8,128)(2,1)S(1)} %collective-permute-done.1.refs_1_, bf16[32,4096]{1,0:T(8,128)(2,1)S(1)} %collective-permute-done.5.refs_2_, bf16[32,4096]{1,0:T(8,128)(2,1)S(1)} %collective-permute-done.6.refs_3_, ...), custom_call_target="tpu_custom_call" | custom-call | flops 1024 | bytes 1024 | tf_op jit(solution)/shard_map/pallas_call | solution.py:107
  24.7 1.3 %collective-permute-start.7 = (bf16[128,512]{1,0:T(8,128)(2,1)S(1)}, bf16[128,512]{1,0:T(8,128)(2,1)S(1)}, u32[]{:S(2)}, u32[]{:S(2)}) collective-permute-start(bf16[128,512]{1,0:T(8,128)(2,1)S(1)} %shard_map.57.refs_0_), channel_id=1, source_target_pairs={{0,16},{8,24},{1,17},{9,25},{2,18},{10,26},{3,19},{11,27},{4,20},{... | collective-permute-start | bytes 393224 | tf_op jit(solution)/shard_map/ppermute | solution.py:25
  26.0 3.5 %collective-permute-start.12 = (bf16[128,512]{1,0:T(8,128)(2,1)S(1)}, bf16[128,512]{1,0:T(8,128)(2,1)S(1)}, u32[]{:S(2)}, u32[]{:S(2)}) collective-permute-start(bf16[128,512]{1,0:T(8,128)(2,1)S(1)} %shard_map.56.refs_0_), channel_id=1, source_target_pairs={{0,8},{8,16},{16,24},{1,9},{9,17},{17,25},{2,10},{10,18},{18,26},{... | collective-permute-start | bytes 393224 | tf_op jit(solution)/shard_map/ppermute | solution.py:25
  29.5 1.9 %collective-permute-start.11 = (bf16[128,512]{1,0:T(8,128)(2,1)S(1)}, bf16[128,512]{1,0:T(8,128)(2,1)S(1)}, u32[]{:S(2)}, u32[]{:S(2)}) collective-permute-start(bf16[128,512]{1,0:T(8,128)(2,1)S(1)} %shard_map.57.refs_0_), channel_id=1, source_target_pairs={{0,8},{8,16},{16,24},{1,9},{9,17},{17,25},{2,10},{10,18},{18,26},{... | collective-permute-start | bytes 393224 | tf_op jit(solution)/shard_map/ppermute | solution.py:25
  31.4 6.3 %shard_map.58 = (bf16[512,4096]{1,0:T(8,128)(2,1)S(1)}, bf16[512,4096]{1,0:T(8,128)(2,1)S(1)}, bf16[512,4096]{1,0:T(8,128)(2,1)S(1)}, bf16[512,4096]{1,0:T(8,128)(2,1)S(1)}) custom-call(s32[1]{0:T(128)} %bitcast.3.target_ref, bf16[4,512,4096]{2,1,0:T(8,128)(2,1)} %bitcast.9), custom_call_target="tpu_custom_call" | custom-call | flops 1024 | bytes 1024 | tf_op jit(solution)/shard_map/pallas_call | solution.py:85
  37.7 0.7 %collective-permute-start.10 = (bf16[128,512]{1,0:T(8,128)(2,1)S(1)}, bf16[128,512]{1,0:T(8,128)(2,1)S(1)}, u32[]{:S(2)}, u32[]{:S(2)}) collective-permute-start(bf16[128,512]{1,0:T(8,128)(2,1)S(1)} %collective-permute-done.9.refs_2_), channel_id=1, source_target_pairs={{16,24},{17,25},{18,26},{19,27},{20,28},{21,29},{22,30},{23,31}} | collective-permute-start | bytes 393224 | tf_op jit(solution)/shard_map/ppermute | solution.py:25
  38.4 0.7 %collective-permute-start.8 = (bf16[128,512]{1,0:T(8,128)(2,1)S(1)}, bf16[128,512]{1,0:T(8,128)(2,1)S(1)}, u32[]{:S(2)}, u32[]{:S(2)}) collective-permute-start(bf16[128,512]{1,0:T(8,128)(2,1)S(1)} %collective-permute-done.7.refs_2_), channel_id=1, source_target_pairs={{16,24},{17,25},{18,26},{19,27},{20,28},{21,29},{22,30},{23,31}} | collective-permute-start | bytes 393224 | tf_op jit(solution)/shard_map/ppermute | solution.py:25
  39.1 2.0 %shard_map.60.refs_2_ = f32[128,4096]{1,0:T(8,128)S(1)} custom-call(bf16[128,512]{1,0:T(8,128)(2,1)S(1)} %shard_map.56.refs_0_, bf16[128,512]{1,0:T(8,128)(2,1)S(1)} %collective-permute-done.12.refs_1_, bf16[128,512]{1,0:T(8,128)(2,1)S(1)} %collective-permute-done.9.refs_2_, bf16[512,4096]{1,0:T(8,128)(2,1)S(1)} %get-tuple-element.39.refs_3_, ...), custom_call_target="tpu_custom_call" | custom-call | flops 1024 | bytes 1024 | tf_op jit(solution)/shard_map/pallas_call | solution.py:144
  41.1 2.0 %shard_map.59.refs_2_ = f32[128,4096]{1,0:T(8,128)S(1)} custom-call(bf16[128,512]{1,0:T(8,128)(2,1)S(1)} %shard_map.57.refs_0_, bf16[128,512]{1,0:T(8,128)(2,1)S(1)} %collective-permute-done.11.refs_1_, bf16[128,512]{1,0:T(8,128)(2,1)S(1)} %collective-permute-done.7.refs_2_, bf16[512,4096]{1,0:T(8,128)(2,1)S(1)} %get-tuple-element.39.refs_3_, ...), custom_call_target="tpu_custom_call" | custom-call | flops 1024 | bytes 1024 | tf_op jit(solution)/shard_map/pallas_call | solution.py:144
  43.1 0.9 %shard_map.61 = (f32[64,4096]{1,0:T(8,128)S(1)}, bf16[64,4096]{1,0:T(8,128)(2,1)S(1)}) custom-call(bf16[128,512]{1,0:T(8,128)(2,1)S(1)} %collective-permute-done.10.refs_0_, bf16[512,4096]{1,0:T(8,128)(2,1)S(1)} %get-tuple-element.48.refs_1_, f32[128,4096]{1,0:T(8,128)S(1)} %shard_map.60.refs_2_), custom_call_target="tpu_custom_call" | custom-call | flops 1024 | bytes 1024 | tf_op jit(solution)/shard_map/pallas_call | solution.py:144
  44.1 0.9 %shard_map.62 = (f32[64,4096]{1,0:T(8,128)S(1)}, bf16[64,4096]{1,0:T(8,128)(2,1)S(1)}) custom-call(bf16[128,512]{1,0:T(8,128)(2,1)S(1)} %collective-permute-done.8.refs_0_, bf16[512,4096]{1,0:T(8,128)(2,1)S(1)} %get-tuple-element.48.refs_1_, f32[128,4096]{1,0:T(8,128)S(1)} %shard_map.59.refs_2_), custom_call_target="tpu_custom_call" | custom-call | flops 1024 | bytes 1024 | tf_op jit(solution)/shard_map/pallas_call | solution.py:144
  45.0 0.6 collective-permute-start.13
  45.6 0.4 collective-permute-done.14
  46.0 0.1 add_convert_fusion
  46.1 0.8 %collective-permute-start.16 = (bf16[32,4096]{1,0:T(8,128)(2,1)S(1)}, bf16[32,4096]{1,0:T(8,128)(2,1)S(1)}, u32[]{:S(2)}, u32[]{:S(2)}) collective-permute-start(bf16[32,4096]{1,0:T(8,128)(2,1)S(1)} %get-tuple-element.58), channel_id=1, source_target_pairs={{0,4},{1,3},{2,6},{3,1},{4,0},{5,7},{6,2},{7,5},{8,12},{9,11},{10,... | collective-permute-start | bytes 786440 | tf_op jit(solution)/shard_map/ppermute | solution.py:20
  46.9 1.3 %collective-permute-start.15 = (bf16[32,4096]{1,0:T(8,128)(2,1)S(1)}, bf16[32,4096]{1,0:T(8,128)(2,1)S(1)}, u32[]{:S(2)}, u32[]{:S(2)}) collective-permute-start(bf16[32,4096]{1,0:T(8,128)(2,1)S(1)} %get-tuple-element.57), channel_id=1, source_target_pairs={{0,4},{1,3},{2,6},{3,1},{4,0},{5,7},{6,2},{7,5},{8,12},{9,11},{10,... | collective-permute-start | bytes 786440 | tf_op jit(solution)/shard_map/ppermute | solution.py:20
  48.2 0.1 convert_add_fusion
  48.3 4.2 %collective-permute-done.16 = bf16[32,4096]{1,0:T(8,128)(2,1)S(1)} collective-permute-done((bf16[32,4096]{1,0:T(8,128)(2,1)S(1)}, bf16[32,4096]{1,0:T(8,128)(2,1)S(1)}, u32[]{:S(2)}, u32[]{:S(2)}) %collective-permute-start.16) | collective-permute-done | bytes 262176 | tf_op jit(solution)/shard_map/ppermute | solution.py:20
  52.6 1.5 %collective-permute-start.17 = (bf16[32,4096]{1,0:T(8,128)(2,1)S(1)}, bf16[32,4096]{1,0:T(8,128)(2,1)S(1)}, u32[]{:S(2)}, u32[]{:S(2)}) collective-permute-start(bf16[32,4096]{1,0:T(8,128)(2,1)S(1)} %fusion), channel_id=1, source_target_pairs={{0,2},{1,5},{2,0},{3,7},{4,6},{5,1},{6,4},{7,3},{8,10},{9,13},{10,... | collective-permute-start | bytes 786440 | tf_op jit(solution)/shard_map/ppermute | solution.py:20
  54.2 2.0 %collective-permute-done.15 = bf16[32,4096]{1,0:T(8,128)(2,1)S(1)} collective-permute-done((bf16[32,4096]{1,0:T(8,128)(2,1)S(1)}, bf16[32,4096]{1,0:T(8,128)(2,1)S(1)}, u32[]{:S(2)}, u32[]{:S(2)}) %collective-permute-start.15) | collective-permute-done | bytes 262176 | tf_op jit(solution)/shard_map/ppermute | solution.py:20
  56.1 2.9 %collective-permute-done.17 = bf16[32,4096]{1,0:T(8,128)(2,1)S(1)} collective-permute-done((bf16[32,4096]{1,0:T(8,128)(2,1)S(1)}, bf16[32,4096]{1,0:T(8,128)(2,1)S(1)}, u32[]{:S(2)}, u32[]{:S(2)}) %collective-permute-start.17) | collective-permute-done | bytes 262176 | tf_op jit(solution)/shard_map/ppermute | solution.py:20
  59.1 0.8 %fusion.4 = bf16[1,32,4096]{2,1,0:T(8,128)(2,1)} fusion(bf16[32,4096]{1,0:T(8,128)(2,1)S(1)} %collective-permute-done.17, bf16[32,4096]{1,0:T(8,128)(2,1)S(1)} %collective-permute-done.15, f32[64,4096]{1,0:T(8,128)S(1)} %convert_add_fusion, bf16[1,32,4096]{2,1,0:T(8,128)(2,1)S(1)} %copy-done.1), kind=kLoop, calls=%fused_computation.8 | loop fusion | flops 917504 | bytes 1572864 | tf_op jit(solution)/shard_map/broadcast_in_dim | solution.py:195
  (21 shorter events, 0.3 us)
Async XLA Ops:
  0.0 16.2 %copy-start = (bf16[1,32,4096]{2,1,0:T(8,128)(2,1)S(1)}, bf16[1,32,4096]{2,1,0:T(8,128)(2,1)}, u32[]{:S(2)}) copy-start(bf16[1,32,4096]{2,1,0:T(8,128)(2,1)} %param.5) | copy-start | bytes 786436
  0.0 9.9 %collective-permute-start.1 = (bf16[32,4096]{1,0:T(8,128)(2,1)}, bf16[32,4096]{1,0:T(8,128)(2,1)S(1)}, u32[]{:S(2)}, u32[]{:S(2)}) collective-permute-start(bf16[32,4096]{1,0:T(8,128)(2,1)} %bitcast.11), channel_id=1, source_target_pairs={{0,2},{1,5},{2,0},{3,7},{4,6},{5,1},{6,4},{7,3},{8,10},{9,13},{10,... | collective-permute-start | bytes 786440 | tf_op jit(solution)/shard_map/ppermute | solution.py:20
  2.9 8.4 %collective-permute-start = (bf16[32,4096]{1,0:T(8,128)(2,1)}, bf16[32,4096]{1,0:T(8,128)(2,1)S(1)}, u32[]{:S(2)}, u32[]{:S(2)}) collective-permute-start(bf16[32,4096]{1,0:T(8,128)(2,1)} %bitcast.12), channel_id=1, source_target_pairs={{0,4},{1,3},{2,6},{3,1},{4,0},{5,7},{6,2},{7,5},{8,12},{9,11},{10,... | collective-permute-start | bytes 786440 | tf_op jit(solution)/shard_map/ppermute | solution.py:20
  9.9 6.4 %collective-permute-start.2 = (bf16[32,4096]{1,0:T(8,128)(2,1)S(1)}, bf16[32,4096]{1,0:T(8,128)(2,1)S(1)}, u32[]{:S(2)}, u32[]{:S(2)}) collective-permute-start(bf16[32,4096]{1,0:T(8,128)(2,1)S(1)} %collective-permute-done.1.refs_1_), channel_id=1, source_target_pairs={{0,4},{1,3},{2,6},{3,1},{4,0},{5,7},{6,2},{7,5},{8,12},{9,11},{10,... | collective-permute-start | bytes 786440 | tf_op jit(solution)/shard_map/ppermute | solution.py:20
  13.6 3.2 %collective-permute-start.3 = (bf16[32,4096]{1,0:T(8,128)(2,1)S(1)}, bf16[32,4096]{1,0:T(8,128)(2,1)S(1)}, u32[]{:S(2)}, u32[]{:S(2)}) collective-permute-start(bf16[32,4096]{1,0:T(8,128)(2,1)S(1)} %collective-permute-done.refs_0_), channel_id=1, source_target_pairs={{0,1},{1,0},{2,3},{3,2},{4,5},{5,4},{6,7},{7,6},{8,9},{9,8},{10,11... | collective-permute-start | bytes 786440 | tf_op jit(solution)/shard_map/ppermute | solution.py:20
  16.2 1.5 %collective-permute-start.4 = (bf16[32,4096]{1,0:T(8,128)(2,1)S(1)}, bf16[32,4096]{1,0:T(8,128)(2,1)S(1)}, u32[]{:S(2)}, u32[]{:S(2)}) collective-permute-start(bf16[32,4096]{1,0:T(8,128)(2,1)S(1)} %collective-permute-done.2.refs_1_), channel_id=1, source_target_pairs={{0,1},{1,0},{2,3},{3,2},{4,5},{5,4},{6,7},{7,6},{8,9},{9,8},{10,11... | collective-permute-start | bytes 786440 | tf_op jit(solution)/shard_map/ppermute | solution.py:20
  16.2 7.7 %collective-permute-start.5 = (bf16[32,4096]{1,0:T(8,128)(2,1)S(1)}, bf16[32,4096]{1,0:T(8,128)(2,1)S(1)}, u32[]{:S(2)}, u32[]{:S(2)}) collective-permute-start(bf16[32,4096]{1,0:T(8,128)(2,1)S(1)} %bitcast.14), channel_id=1, source_target_pairs={{0,1},{1,0},{2,3},{3,2},{4,5},{5,4},{6,7},{7,6},{8,9},{9,8},{10,11... | collective-permute-start | bytes 786440 | tf_op jit(solution)/shard_map/ppermute | solution.py:20
  16.8 7.2 %collective-permute-start.6 = (bf16[32,4096]{1,0:T(8,128)(2,1)S(1)}, bf16[32,4096]{1,0:T(8,128)(2,1)S(1)}, u32[]{:S(2)}, u32[]{:S(2)}) collective-permute-start(bf16[32,4096]{1,0:T(8,128)(2,1)S(1)} %collective-permute-done.1.refs_1_), channel_id=1, source_target_pairs={{0,1},{1,0},{2,3},{3,2},{4,5},{5,4},{6,7},{7,6},{8,9},{9,8},{10,11... | collective-permute-start | bytes 786440 | tf_op jit(solution)/shard_map/ppermute | solution.py:20
  18.5 19.2 %collective-permute-start.9 = (bf16[128,512]{1,0:T(8,128)(2,1)S(1)}, bf16[128,512]{1,0:T(8,128)(2,1)S(1)}, u32[]{:S(2)}, u32[]{:S(2)}) collective-permute-start(bf16[128,512]{1,0:T(8,128)(2,1)S(1)} %shard_map.56.refs_0_), channel_id=1, source_target_pairs={{0,16},{8,24},{1,17},{9,25},{2,18},{10,26},{3,19},{11,27},{4,20},{... | collective-permute-start | bytes 393224 | tf_op jit(solution)/shard_map/ppermute | solution.py:25
  24.7 13.7 %collective-permute-start.7 = (bf16[128,512]{1,0:T(8,128)(2,1)S(1)}, bf16[128,512]{1,0:T(8,128)(2,1)S(1)}, u32[]{:S(2)}, u32[]{:S(2)}) collective-permute-start(bf16[128,512]{1,0:T(8,128)(2,1)S(1)} %shard_map.57.refs_0_), channel_id=1, source_target_pairs={{0,16},{8,24},{1,17},{9,25},{2,18},{10,26},{3,19},{11,27},{4,20},{... | collective-permute-start | bytes 393224 | tf_op jit(solution)/shard_map/ppermute | solution.py:25
  26.0 13.1 %collective-permute-start.12 = (bf16[128,512]{1,0:T(8,128)(2,1)S(1)}, bf16[128,512]{1,0:T(8,128)(2,1)S(1)}, u32[]{:S(2)}, u32[]{:S(2)}) collective-permute-start(bf16[128,512]{1,0:T(8,128)(2,1)S(1)} %shard_map.56.refs_0_), channel_id=1, source_target_pairs={{0,8},{8,16},{16,24},{1,9},{9,17},{17,25},{2,10},{10,18},{18,26},{... | collective-permute-start | bytes 393224 | tf_op jit(solution)/shard_map/ppermute | solution.py:25
  29.5 11.6 %collective-permute-start.11 = (bf16[128,512]{1,0:T(8,128)(2,1)S(1)}, bf16[128,512]{1,0:T(8,128)(2,1)S(1)}, u32[]{:S(2)}, u32[]{:S(2)}) collective-permute-start(bf16[128,512]{1,0:T(8,128)(2,1)S(1)} %shard_map.57.refs_0_), channel_id=1, source_target_pairs={{0,8},{8,16},{16,24},{1,9},{9,17},{17,25},{2,10},{10,18},{18,26},{... | collective-permute-start | bytes 393224 | tf_op jit(solution)/shard_map/ppermute | solution.py:25
  37.7 5.4 %collective-permute-start.10 = (bf16[128,512]{1,0:T(8,128)(2,1)S(1)}, bf16[128,512]{1,0:T(8,128)(2,1)S(1)}, u32[]{:S(2)}, u32[]{:S(2)}) collective-permute-start(bf16[128,512]{1,0:T(8,128)(2,1)S(1)} %collective-permute-done.9.refs_2_), channel_id=1, source_target_pairs={{16,24},{17,25},{18,26},{19,27},{20,28},{21,29},{22,30},{23,31}} | collective-permute-start | bytes 393224 | tf_op jit(solution)/shard_map/ppermute | solution.py:25
  38.4 4.7 %collective-permute-start.8 = (bf16[128,512]{1,0:T(8,128)(2,1)S(1)}, bf16[128,512]{1,0:T(8,128)(2,1)S(1)}, u32[]{:S(2)}, u32[]{:S(2)}) collective-permute-start(bf16[128,512]{1,0:T(8,128)(2,1)S(1)} %collective-permute-done.7.refs_2_), channel_id=1, source_target_pairs={{16,24},{17,25},{18,26},{19,27},{20,28},{21,29},{22,30},{23,31}} | collective-permute-start | bytes 393224 | tf_op jit(solution)/shard_map/ppermute | solution.py:25
  44.0 2.0 %collective-permute-start.14 = (bf16[64,4096]{1,0:T(8,128)(2,1)S(1)}, bf16[64,4096]{1,0:T(8,128)(2,1)S(1)}, u32[]{:S(2)}, u32[]{:S(2)}) collective-permute-start(bf16[64,4096]{1,0:T(8,128)(2,1)S(1)} %get-tuple-element.52), channel_id=1, source_target_pairs={{0,1},{1,0},{2,3},{3,2},{4,5},{5,4},{6,7},{7,6},{8,9},{9,8},{10,11... | collective-permute-start | bytes 1572872 | tf_op jit(solution)/shard_map/ppermute | solution.py:20
  45.0 14.0 %copy-start.1 = (bf16[1,32,4096]{2,1,0:T(8,128)(2,1)S(1)}, bf16[1,32,4096]{2,1,0:T(8,128)(2,1)}, u32[]{:S(2)}) copy-start(bf16[1,32,4096]{2,1,0:T(8,128)(2,1)} %param.6) | copy-start | bytes 786436
  45.0 3.2 %collective-permute-start.13 = (bf16[64,4096]{1,0:T(8,128)(2,1)S(1)}, bf16[64,4096]{1,0:T(8,128)(2,1)S(1)}, u32[]{:S(2)}, u32[]{:S(2)}) collective-permute-start(bf16[64,4096]{1,0:T(8,128)(2,1)S(1)} %get-tuple-element.55), channel_id=1, source_target_pairs={{0,1},{1,0},{2,3},{3,2},{4,5},{5,4},{6,7},{7,6},{8,9},{9,8},{10,11... | collective-permute-start | bytes 1572872 | tf_op jit(solution)/shard_map/ppermute | solution.py:20
  46.1 6.4 %collective-permute-start.16 = (bf16[32,4096]{1,0:T(8,128)(2,1)S(1)}, bf16[32,4096]{1,0:T(8,128)(2,1)S(1)}, u32[]{:S(2)}, u32[]{:S(2)}) collective-permute-start(bf16[32,4096]{1,0:T(8,128)(2,1)S(1)} %get-tuple-element.58), channel_id=1, source_target_pairs={{0,4},{1,3},{2,6},{3,1},{4,0},{5,7},{6,2},{7,5},{8,12},{9,11},{10,... | collective-permute-start | bytes 786440 | tf_op jit(solution)/shard_map/ppermute | solution.py:20
  46.9 9.2 %collective-permute-start.15 = (bf16[32,4096]{1,0:T(8,128)(2,1)S(1)}, bf16[32,4096]{1,0:T(8,128)(2,1)S(1)}, u32[]{:S(2)}, u32[]{:S(2)}) collective-permute-start(bf16[32,4096]{1,0:T(8,128)(2,1)S(1)} %get-tuple-element.57), channel_id=1, source_target_pairs={{0,4},{1,3},{2,6},{3,1},{4,0},{5,7},{6,2},{7,5},{8,12},{9,11},{10,... | collective-permute-start | bytes 786440 | tf_op jit(solution)/shard_map/ppermute | solution.py:20
  52.6 6.4 %collective-permute-start.17 = (bf16[32,4096]{1,0:T(8,128)(2,1)S(1)}, bf16[32,4096]{1,0:T(8,128)(2,1)S(1)}, u32[]{:S(2)}, u32[]{:S(2)}) collective-permute-start(bf16[32,4096]{1,0:T(8,128)(2,1)S(1)} %fusion), channel_id=1, source_target_pairs={{0,2},{1,5},{2,0},{3,7},{4,6},{5,1},{6,4},{7,3},{8,10},{9,13},{10,... | collective-permute-start | bytes 786440 | tf_op jit(solution)/shard_map/ppermute | solution.py:20

commit v3 on v2

--- a/solution.py
+++ b/solution.py
@@ -81,7 +81,7 @@
 
 def pick(weights, target):
     count, depth, wide = weights.shape
-    cuts = 2
+    cuts = 4
     return pl.pallas_call(
         functools.partial(pick_kernel, cuts),
         in_specs=[SCALAR, FAR],
@@ -142,7 +142,7 @@
     summed = acc is not None
     halves = [pltpu.VMEM((rows // 2, wide), F32), pltpu.VMEM((rows // 2, wide), BF16)]
     return pl.pallas_call(
-        functools.partial(decode_kernel, count, tile_of(wide, 2048), summed, halved),
+        functools.partial(decode_kernel, count, tile_of(wide, 4096), summed, halved),
         in_specs=[WHOLE] * (2 * count + summed),
         out_specs=[WHOLE, WHOLE] if halved else WHOLE,
         out_shape=halves if halved else pltpu.VMEM((rows, wide), F32),
@@ -158,33 +158,31 @@
     bits = [1 << bit for bit in range(1, peers.bit_length() - 1)]
     steps = list(zip(bits, bits[::-1]))
 
+    encoder, bias, mine = load([enc_w[0], enc_b, resid[0]], [4, 1, 1])
     pieces = [resid[0]]
-    for masks in steps:
-        pieces += [swap(piece, masks) for piece in pieces]
-    count = len(pieces)
-    half = count // 2
-    encoder, bias, mine = load([after(enc_w[0], pieces[half]), enc_b, resid[0]], [4, 1, 1])
-    pieces[-1] = after(pieces[-1], encoder)
-    mates = [swap(piece, (1, 1)) for piece in pieces]
+    for step, masks in enumerate(steps):
+        pieces += [swap(piece, masks) for piece in ([mine] + pieces[1:] if step else pieces)]
     pieces[0] = mine
-
-    def gather(group, *gate):
-        return encode([after(pieces[i], *gate) for i in group] + [mates[i] for i in group], encoder, bias)
-
-    def lift(held, *gate):
-        for j in range(len(held), layers):
-            held.append(up(after(held[j - 1], *gate) if j > 2 else held[j - 1], 1, j) if j % 2 else up(held[j - 2], 2, j))
-
-    far = [gather(range(half, count))]
-    near = [gather(range(half), far[0])]
-    weights = pick(after(dec_w[0], near[0]), target)
-    lift(far, weights[0])
-    lift(near, weights[0])
-    sums = [decode([after(lat, near[2]) for lat in held[:-1]], weights[:-1]) for held in (far, near)]
-    top, low = decode([after(far[-1], near[-1], sums[1])], weights[-1:], sums[0], True)
+    half = len(pieces) // 2
+
+    mates = [swap(piece, (1, 1)) for piece in pieces[:half]]
+    near = [encode(pieces[:half] + mates, encoder, bias)]
+    mates = [swap(piece, (1, 1)) for piece in pieces[half:]]
+    far = [encode(pieces[half:] + [after(mates[0], near[0])] + mates[1:], encoder, bias)]
+    weights = pick(after(dec_w[0], far[0]), target)
+    for held in (near, far):
+        for j in range(1, layers):
+            if j % 2:
+                held.append(up(held[-1] if j == 1 else after(held[-1], weights[0]), 1, j))
+            else:
+                held.append(up(held[j - 2], 2, j))
+
+    near_sum = decode(near[:-1], weights[:-1])
+    far_sum = decode([after(lat, far[-2]) for lat in far[:-1]], weights[:-1])
+    top, low = decode(near[-1:], weights[-1:], near_sum, True)
     ends = [top + swap(low, (1, 1)).astype(F32)]
-    top, low = decode([after(near[-1], low)], weights[-1:], sums[1], True)
-    ends.insert(0, top + swap(low, (1, 1)).astype(F32))
+    top, low = decode([after(far[-1], low)], weights[-1:], far_sum, True)
+    ends.append(top + swap(low, (1, 1)).astype(F32))
     each = resid.shape[1]
     totals = [end[i * each : (i + 1) * each] for end in ends for i in range(half)]
     for masks in steps[::-1]:

time: 60.1 us -> 57.5 us (0.957)
  waiting for transfers between devices: 18.6 us -> 14.6 us
  starting transfers between devices: 24.1 us -> 25.9 us
  Pallas kernels: 15.9 us -> 15.2 us
    ppermute x12, waiting for transfers between devices: 18.6 us -> 14.6 us  [swap(): lax.ppermute(shard, 'latent', [(i, i ^ masks[i & 1]) for i in range(peers)])]
    ppermute x12, starting transfers between devices: 10.7 us -> 13.6 us  [swap(): lax.ppermute(shard, 'latent', [(i, i ^ masks[i & 1]) for i in range(peers)])]
    ppermute x6, starting transfers between devices: 13.4 us -> 12.3 us  [up(): lax.ppermute(shard, 'layer', [(i - by, i) for i in range(back, layers)])]
    pallas_call x4, Pallas kernels: 5.8 us -> 5.05 us  [decode(): pl.pallas_call(functools.partial(decode_kernel, count, tile_of(wide, 4096...]
  transfers between devices with their start and end apart: 18 -> 18, of which waited for: 7 -> 6; matrix products, arithmetic and copies ran while one was open for 0% -> 0% of each run, Pallas kernels for 25% -> 25%
where the time goes in v3:
time: 57.5 us; the launch traced here: 57 us
  starting transfers between devices  25.9 us (45%)
  Pallas kernels  15.2 us (26%)
  waiting for transfers between devices  14.6 us (25%)
  other arithmetic  1.04 us (2%)
    ppermute x12, waiting for transfers between devices, swap(): lax.ppermute(shard, 'latent', [(i, i ^ masks[i & 1]) for i in range(peers)])  14.6 us
    ppermute x12, starting transfers between devices, swap(): lax.ppermute(shard, 'latent', [(i, i ^ masks[i & 1]) for i in range(peers)])  13.6 us
    ppermute x6, starting transfers between devices, up(): lax.ppermute(shard, 'layer', [(i - by, i) for i in range(back, layers)])  12.3 us
    pallas_call x1, Pallas kernels, pick(): pl.pallas_call(functools.partial(pick_kernel, cuts), in_specs=[SCALAR, FA...  6.33 us
    pallas_call x4, Pallas kernels, decode(): pl.pallas_call(functools.partial(decode_kernel, count, tile_of(wide, 4096...  5.05 us
    pallas_call x1, Pallas kernels, load(): pl.pallas_call(functools.partial(load_kernel, count, cuts), in_specs=[FAR...  2.28 us
    pallas_call x2, Pallas kernels, encode(): pl.pallas_call(functools.partial(encode_kernel, count), in_specs=[WHOLE]...  1.52 us
  transfers between devices with their start and end apart: 18, of which 6 were waited for; matrix products, arithmetic and copies ran while one was open for 0% of the time, Pallas kernels for 25%

profile of v3, /device:TPU:0, one launch (start us, length us, event | category | flops | bytes accessed | tf_op | source)
XLA Modules:
  0.0 57.0 jit_solution(9305616829019657473)
XLA Ops:
  0.0 2.9 %collective-permute-start = (bf16[32,4096]{1,0:T(8,128)(2,1)}, bf16[32,4096]{1,0:T(8,128)(2,1)S(1)}, u32[]{:S(2)}, u32[]{:S(2)}) collective-permute-start(bf16[32,4096]{1,0:T(8,128)(2,1)} %bitcast.11), channel_id=1, source_target_pairs={{0,2},{1,5},{2,0},{3,7},{4,6},{5,1},{6,4},{7,3},{8,10},{9,13},{10,... | collective-permute-start | bytes 786440 | tf_op jit(solution)/shard_map/ppermute | solution.py:20
  2.9 2.3 %shard_map.55 = (bf16[4096,512]{1,0:T(8,128)(2,1)S(1)}, f32[1,512]{1,0:T(1,128)S(1)}, bf16[32,4096]{1,0:T(8,128)(2,1)S(1)}) custom-call(bf16[4096,512]{1,0:T(8,128)(2,1)} %bitcast.10, f32[1,512]{1,0:T(1,128)} %refs_1_.1, bf16[32,4096]{1,0:T(8,128)(2,1)} %bitcast.12), custom_call_target="tpu_custom_call" | custom-call | flops 1024 | bytes 1024 | tf_op jit(solution)/shard_map/pallas_call | solution.py:59
  5.2 1.6 %collective-permute-start.4 = (bf16[32,4096]{1,0:T(8,128)(2,1)S(1)}, bf16[32,4096]{1,0:T(8,128)(2,1)S(1)}, u32[]{:S(2)}, u32[]{:S(2)}) collective-permute-start(bf16[32,4096]{1,0:T(8,128)(2,1)S(1)} %get-tuple-element.24.refs_0_), channel_id=1, source_target_pairs={{0,4},{1,3},{2,6},{3,1},{4,0},{5,7},{6,2},{7,5},{8,12},{9,11},{10,... | collective-permute-start | bytes 786440 | tf_op jit(solution)/shard_map/ppermute | solution.py:20
  6.8 0.8 %collective-permute-done.refs_1_ = bf16[32,4096]{1,0:T(8,128)(2,1)S(1)} collective-permute-done((bf16[32,4096]{1,0:T(8,128)(2,1)}, bf16[32,4096]{1,0:T(8,128)(2,1)S(1)}, u32[]{:S(2)}, u32[]{:S(2)}) %collective-permute-start) | collective-permute-done | bytes 262176 | tf_op jit(solution)/shard_map/ppermute | solution.py:20
  7.6 3.7 %collective-permute-start.5 = (bf16[32,4096]{1,0:T(8,128)(2,1)S(1)}, bf16[32,4096]{1,0:T(8,128)(2,1)S(1)}, u32[]{:S(2)}, u32[]{:S(2)}) collective-permute-start(bf16[32,4096]{1,0:T(8,128)(2,1)S(1)} %collective-permute-done.refs_1_), channel_id=1, source_target_pairs={{0,4},{1,3},{2,6},{3,1},{4,0},{5,7},{6,2},{7,5},{8,12},{9,11},{10,... | collective-permute-start | bytes 786440 | tf_op jit(solution)/shard_map/ppermute | solution.py:20
  11.3 0.5 collective-permute-start.2
  11.9 3.8 %collective-permute-done.5.refs_1_ = bf16[32,4096]{1,0:T(8,128)(2,1)S(1)} collective-permute-done((bf16[32,4096]{1,0:T(8,128)(2,1)S(1)}, bf16[32,4096]{1,0:T(8,128)(2,1)S(1)}, u32[]{:S(2)}, u32[]{:S(2)}) %collective-permute-start.5) | collective-permute-done | bytes 262176 | tf_op jit(solution)/shard_map/ppermute | solution.py:20
  15.7 0.8 %shard_map.56.refs_0_ = bf16[128,512]{1,0:T(8,128)(2,1)S(1)} custom-call(bf16[32,4096]{1,0:T(8,128)(2,1)S(1)} %get-tuple-element.24.refs_0_, bf16[32,4096]{1,0:T(8,128)(2,1)S(1)} %collective-permute-done.refs_1_, bf16[32,4096]{1,0:T(8,128)(2,1)S(1)} %collective-permute-done.1.refs_2_, bf16[32,4096]{1,0:T(8,128)(2,1)S(1)} %collective-permute-done.2.refs_3_, ...), custom_call_target="tpu_custom_call" | custom-call | flops 1024 | bytes 1024 | tf_op jit(solution)/shard_map/pallas_call | solution.py:107
  16.5 4.2 %collective-permute-start.3 = (bf16[128,512]{1,0:T(8,128)(2,1)S(1)}, bf16[128,512]{1,0:T(8,128)(2,1)S(1)}, u32[]{:S(2)}, u32[]{:S(2)}) collective-permute-start(bf16[128,512]{1,0:T(8,128)(2,1)S(1)} %shard_map.56.refs_0_), channel_id=1, source_target_pairs={{0,16},{8,24},{1,17},{9,25},{2,18},{10,26},{3,19},{11,27},{4,20},{... | collective-permute-start | bytes 393224 | tf_op jit(solution)/shard_map/ppermute | solution.py:25
  20.8 0.8 %shard_map.57.refs_0_ = bf16[128,512]{1,0:T(8,128)(2,1)S(1)} custom-call(bf16[32,4096]{1,0:T(8,128)(2,1)S(1)} %collective-permute-done.4.refs_0_, bf16[32,4096]{1,0:T(8,128)(2,1)S(1)} %collective-permute-done.5.refs_1_, bf16[32,4096]{1,0:T(8,128)(2,1)S(1)} %collective-permute-done.6.refs_2_, bf16[32,4096]{1,0:T(8,128)(2,1)S(1)} %collective-permute-done.7.refs_3_, ...), custom_call_target="tpu_custom_call" | custom-call | flops 1024 | bytes 1024 | tf_op jit(solution)/shard_map/pallas_call | solution.py:107
  21.5 1.3 %collective-permute-start.11 = (bf16[128,512]{1,0:T(8,128)(2,1)S(1)}, bf16[128,512]{1,0:T(8,128)(2,1)S(1)}, u32[]{:S(2)}, u32[]{:S(2)}) collective-permute-start(bf16[128,512]{1,0:T(8,128)(2,1)S(1)} %shard_map.57.refs_0_), channel_id=1, source_target_pairs={{0,16},{8,24},{1,17},{9,25},{2,18},{10,26},{3,19},{11,27},{4,20},{... | collective-permute-start | bytes 393224 | tf_op jit(solution)/shard_map/ppermute | solution.py:25
  22.8 3.5 %collective-permute-start.9 = (bf16[128,512]{1,0:T(8,128)(2,1)S(1)}, bf16[128,512]{1,0:T(8,128)(2,1)S(1)}, u32[]{:S(2)}, u32[]{:S(2)}) collective-permute-start(bf16[128,512]{1,0:T(8,128)(2,1)S(1)} %shard_map.56.refs_0_), channel_id=1, source_target_pairs={{0,8},{8,16},{16,24},{1,9},{9,17},{17,25},{2,10},{10,18},{18,26},{... | collective-permute-start | bytes 393224 | tf_op jit(solution)/shard_map/ppermute | solution.py:25
  26.3 1.9 %collective-permute-start.13 = (bf16[128,512]{1,0:T(8,128)(2,1)S(1)}, bf16[128,512]{1,0:T(8,128)(2,1)S(1)}, u32[]{:S(2)}, u32[]{:S(2)}) collective-permute-start(bf16[128,512]{1,0:T(8,128)(2,1)S(1)} %shard_map.57.refs_0_), channel_id=1, source_target_pairs={{0,8},{8,16},{16,24},{1,9},{9,17},{17,25},{2,10},{10,18},{18,26},{... | collective-permute-start | bytes 393224 | tf_op jit(solution)/shard_map/ppermute | solution.py:25
  28.2 6.3 %shard_map.58 = (bf16[512,4096]{1,0:T(8,128)(2,1)S(1)}, bf16[512,4096]{1,0:T(8,128)(2,1)S(1)}, bf16[512,4096]{1,0:T(8,128)(2,1)S(1)}, bf16[512,4096]{1,0:T(8,128)(2,1)S(1)}) custom-call(s32[1]{0:T(128)} %bitcast.3.target_ref, bf16[4,512,4096]{2,1,0:T(8,128)(2,1)} %bitcast.9), custom_call_target="tpu_custom_call" | custom-call | flops 1024 | bytes 1024 | tf_op jit(solution)/shard_map/pallas_call | solution.py:85
  34.6 0.7 %collective-permute-start.8 = (bf16[128,512]{1,0:T(8,128)(2,1)S(1)}, bf16[128,512]{1,0:T(8,128)(2,1)S(1)}, u32[]{:S(2)}, u32[]{:S(2)}) collective-permute-start(bf16[128,512]{1,0:T(8,128)(2,1)S(1)} %collective-permute-done.3.refs_2_), channel_id=1, source_target_pairs={{16,24},{17,25},{18,26},{19,27},{20,28},{21,29},{22,30},{23,31}} | collective-permute-start | bytes 393224 | tf_op jit(solution)/shard_map/ppermute | solution.py:25
  35.3 0.7 %collective-permute-start.12 = (bf16[128,512]{1,0:T(8,128)(2,1)S(1)}, bf16[128,512]{1,0:T(8,128)(2,1)S(1)}, u32[]{:S(2)}, u32[]{:S(2)}) collective-permute-start(bf16[128,512]{1,0:T(8,128)(2,1)S(1)} %collective-permute-done.11.refs_2_), channel_id=1, source_target_pairs={{16,24},{17,25},{18,26},{19,27},{20,28},{21,29},{22,30},{23,31}} | collective-permute-start | bytes 393224 | tf_op jit(solution)/shard_map/ppermute | solution.py:25
  36.0 1.8 %shard_map.59.refs_2_ = f32[128,4096]{1,0:T(8,128)S(1)} custom-call(bf16[128,512]{1,0:T(8,128)(2,1)S(1)} %shard_map.56.refs_0_, bf16[128,512]{1,0:T(8,128)(2,1)S(1)} %collective-permute-done.9.refs_1_, bf16[128,512]{1,0:T(8,128)(2,1)S(1)} %collective-permute-done.3.refs_2_, bf16[512,4096]{1,0:T(8,128)(2,1)S(1)} %get-tuple-element.29.refs_3_, ...), custom_call_target="tpu_custom_call" | custom-call | flops 1024 | bytes 1024 | tf_op jit(solution)/shard_map/pallas_call | solution.py:144
  37.8 1.8 %shard_map.61.refs_2_ = f32[128,4096]{1,0:T(8,128)S(1)} custom-call(bf16[128,512]{1,0:T(8,128)(2,1)S(1)} %shard_map.57.refs_0_, bf16[128,512]{1,0:T(8,128)(2,1)S(1)} %collective-permute-done.13.refs_1_, bf16[128,512]{1,0:T(8,128)(2,1)S(1)} %collective-permute-done.11.refs_2_, bf16[512,4096]{1,0:T(8,128)(2,1)S(1)} %get-tuple-element.29.refs_3_, ...), custom_call_target="tpu_custom_call" | custom-call | flops 1024 | bytes 1024 | tf_op jit(solution)/shard_map/pallas_call | solution.py:144
  39.6 0.7 %shard_map.60 = (f32[64,4096]{1,0:T(8,128)S(1)}, bf16[64,4096]{1,0:T(8,128)(2,1)S(1)}) custom-call(bf16[128,512]{1,0:T(8,128)(2,1)S(1)} %collective-permute-done.8.refs_0_, bf16[512,4096]{1,0:T(8,128)(2,1)S(1)} %get-tuple-element.31.refs_1_, f32[128,4096]{1,0:T(8,128)S(1)} %shard_map.59.refs_2_), custom_call_target="tpu_custom_call" | custom-call | flops 1024 | bytes 1024 | tf_op jit(solution)/shard_map/pallas_call | solution.py:144
  40.3 0.7 %shard_map.62 = (f32[64,4096]{1,0:T(8,128)S(1)}, bf16[64,4096]{1,0:T(8,128)(2,1)S(1)}) custom-call(bf16[128,512]{1,0:T(8,128)(2,1)S(1)} %collective-permute-done.12.refs_0_, bf16[512,4096]{1,0:T(8,128)(2,1)S(1)} %get-tuple-element.31.refs_1_, f32[128,4096]{1,0:T(8,128)S(1)} %shard_map.61.refs_2_), custom_call_target="tpu_custom_call" | custom-call | flops 1024 | bytes 1024 | tf_op jit(solution)/shard_map/pallas_call | solution.py:144
  41.1 0.1 collective-permute-start.14
  41.2 0.5 collective-permute-start.10
  41.7 1.4 %collective-permute-done.14 = bf16[64,4096]{1,0:T(8,128)(2,1)S(1)} collective-permute-done((bf16[64,4096]{1,0:T(8,128)(2,1)S(1)}, bf16[64,4096]{1,0:T(8,128)(2,1)S(1)}, u32[]{:S(2)}, u32[]{:S(2)}) %collective-permute-start.14) | collective-permute-done | bytes 524320 | tf_op jit(solution)/shard_map/ppermute | solution.py:20
  43.1 0.1 add_convert_fusion
  43.2 2.1 %collective-permute-start.16 = (bf16[32,4096]{1,0:T(8,128)(2,1)S(1)}, bf16[32,4096]{1,0:T(8,128)(2,1)S(1)}, u32[]{:S(2)}, u32[]{:S(2)}) collective-permute-start(bf16[32,4096]{1,0:T(8,128)(2,1)S(1)} %get-tuple-element.44), channel_id=1, source_target_pairs={{0,4},{1,3},{2,6},{3,1},{4,0},{5,7},{6,2},{7,5},{8,12},{9,11},{10,... | collective-permute-start | bytes 786440 | tf_op jit(solution)/shard_map/ppermute | solution.py:20
  45.3 0.1 convert_add_fusion
  45.4 0.6 %collective-permute-start.15 = (bf16[32,4096]{1,0:T(8,128)(2,1)S(1)}, bf16[32,4096]{1,0:T(8,128)(2,1)S(1)}, u32[]{:S(2)}, u32[]{:S(2)}) collective-permute-start(bf16[32,4096]{1,0:T(8,128)(2,1)S(1)} %get-tuple-element.43), channel_id=1, source_target_pairs={{0,4},{1,3},{2,6},{3,1},{4,0},{5,7},{6,2},{7,5},{8,12},{9,11},{10,... | collective-permute-start | bytes 786440 | tf_op jit(solution)/shard_map/ppermute | solution.py:20
  46.0 3.6 %collective-permute-done.16 = bf16[32,4096]{1,0:T(8,128)(2,1)S(1)} collective-permute-done((bf16[32,4096]{1,0:T(8,128)(2,1)S(1)}, bf16[32,4096]{1,0:T(8,128)(2,1)S(1)}, u32[]{:S(2)}, u32[]{:S(2)}) %collective-permute-start.16) | collective-permute-done | bytes 262176 | tf_op jit(solution)/shard_map/ppermute | solution.py:20
  49.7 1.6 %collective-permute-start.17 = (bf16[32,4096]{1,0:T(8,128)(2,1)S(1)}, bf16[32,4096]{1,0:T(8,128)(2,1)S(1)}, u32[]{:S(2)}, u32[]{:S(2)}) collective-permute-start(bf16[32,4096]{1,0:T(8,128)(2,1)S(1)} %fusion), channel_id=1, source_target_pairs={{0,2},{1,5},{2,0},{3,7},{4,6},{5,1},{6,4},{7,3},{8,10},{9,13},{10,... | collective-permute-start | bytes 786440 | tf_op jit(solution)/shard_map/ppermute | solution.py:20
  51.3 1.7 %collective-permute-done.15 = bf16[32,4096]{1,0:T(8,128)(2,1)S(1)} collective-permute-done((bf16[32,4096]{1,0:T(8,128)(2,1)S(1)}, bf16[32,4096]{1,0:T(8,128)(2,1)S(1)}, u32[]{:S(2)}, u32[]{:S(2)}) %collective-permute-start.15) | collective-permute-done | bytes 262176 | tf_op jit(solution)/shard_map/ppermute | solution.py:20
  52.9 3.2 %collective-permute-done.17 = bf16[32,4096]{1,0:T(8,128)(2,1)S(1)} collective-permute-done((bf16[32,4096]{1,0:T(8,128)(2,1)S(1)}, bf16[32,4096]{1,0:T(8,128)(2,1)S(1)}, u32[]{:S(2)}, u32[]{:S(2)}) %collective-permute-start.17) | collective-permute-done | bytes 262176 | tf_op jit(solution)/shard_map/ppermute | solution.py:20
  56.1 0.8 %fusion.4 = bf16[1,32,4096]{2,1,0:T(8,128)(2,1)} fusion(bf16[32,4096]{1,0:T(8,128)(2,1)S(1)} %collective-permute-done.17, bf16[32,4096]{1,0:T(8,128)(2,1)S(1)} %collective-permute-done.15, f32[64,4096]{1,0:T(8,128)S(1)} %convert_add_fusion, bf16[1,32,4096]{2,1,0:T(8,128)(2,1)S(1)} %copy-done), kind=kLoop, calls=%fused_computation.8 | loop fusion | flops 917504 | bytes 1572864 | tf_op jit(solution)/shard_map/broadcast_in_dim | solution.py:193
  (19 shorter events, 0.1 us)
Async XLA Ops:
  0.0 7.6 %collective-permute-start = (bf16[32,4096]{1,0:T(8,128)(2,1)}, bf16[32,4096]{1,0:T(8,128)(2,1)S(1)}, u32[]{:S(2)}, u32[]{:S(2)}) collective-permute-start(bf16[32,4096]{1,0:T(8,128)(2,1)} %bitcast.11), channel_id=1, source_target_pairs={{0,2},{1,5},{2,0},{3,7},{4,6},{5,1},{6,4},{7,3},{8,10},{9,13},{10,... | collective-permute-start | bytes 786440 | tf_op jit(solution)/shard_map/ppermute | solution.py:20
  5.2 6.6 %collective-permute-start.4 = (bf16[32,4096]{1,0:T(8,128)(2,1)S(1)}, bf16[32,4096]{1,0:T(8,128)(2,1)S(1)}, u32[]{:S(2)}, u32[]{:S(2)}) collective-permute-start(bf16[32,4096]{1,0:T(8,128)(2,1)S(1)} %get-tuple-element.24.refs_0_), channel_id=1, source_target_pairs={{0,4},{1,3},{2,6},{3,1},{4,0},{5,7},{6,2},{7,5},{8,12},{9,11},{10,... | collective-permute-start | bytes 786440 | tf_op jit(solution)/shard_map/ppermute | solution.py:20
  7.6 8.1 %collective-permute-start.5 = (bf16[32,4096]{1,0:T(8,128)(2,1)S(1)}, bf16[32,4096]{1,0:T(8,128)(2,1)S(1)}, u32[]{:S(2)}, u32[]{:S(2)}) collective-permute-start(bf16[32,4096]{1,0:T(8,128)(2,1)S(1)} %collective-permute-done.refs_1_), channel_id=1, source_target_pairs={{0,4},{1,3},{2,6},{3,1},{4,0},{5,7},{6,2},{7,5},{8,12},{9,11},{10,... | collective-permute-start | bytes 786440 | tf_op jit(solution)/shard_map/ppermute | solution.py:20
  11.3 4.4 %collective-permute-start.1 = (bf16[32,4096]{1,0:T(8,128)(2,1)S(1)}, bf16[32,4096]{1,0:T(8,128)(2,1)S(1)}, u32[]{:S(2)}, u32[]{:S(2)}) collective-permute-start(bf16[32,4096]{1,0:T(8,128)(2,1)S(1)} %get-tuple-element.24.refs_0_), channel_id=1, source_target_pairs={{0,1},{1,0},{2,3},{3,2},{4,5},{5,4},{6,7},{7,6},{8,9},{9,8},{10,11... | collective-permute-start | bytes 786440 | tf_op jit(solution)/shard_map/ppermute | solution.py:20
  11.3 4.4 %collective-permute-start.2 = (bf16[32,4096]{1,0:T(8,128)(2,1)S(1)}, bf16[32,4096]{1,0:T(8,128)(2,1)S(1)}, u32[]{:S(2)}, u32[]{:S(2)}) collective-permute-start(bf16[32,4096]{1,0:T(8,128)(2,1)S(1)} %collective-permute-done.refs_1_), channel_id=1, source_target_pairs={{0,1},{1,0},{2,3},{3,2},{4,5},{5,4},{6,7},{7,6},{8,9},{9,8},{10,11... | collective-permute-start | bytes 786440 | tf_op jit(solution)/shard_map/ppermute | solution.py:20
  11.9 8.9 %collective-permute-start.6 = (bf16[32,4096]{1,0:T(8,128)(2,1)S(1)}, bf16[32,4096]{1,0:T(8,128)(2,1)S(1)}, u32[]{:S(2)}, u32[]{:S(2)}) collective-permute-start(bf16[32,4096]{1,0:T(8,128)(2,1)S(1)} %collective-permute-done.4.refs_0_), channel_id=1, source_target_pairs={{0,1},{1,0},{2,3},{3,2},{4,5},{5,4},{6,7},{7,6},{8,9},{9,8},{10,11... | collective-permute-start | bytes 786440 | tf_op jit(solution)/shard_map/ppermute | solution.py:20
  15.7 5.1 %collective-permute-start.7 = (bf16[32,4096]{1,0:T(8,128)(2,1)S(1)}, bf16[32,4096]{1,0:T(8,128)(2,1)S(1)}, u32[]{:S(2)}, u32[]{:S(2)}) collective-permute-start(bf16[32,4096]{1,0:T(8,128)(2,1)S(1)} %collective-permute-done.5.refs_1_), channel_id=1, source_target_pairs={{0,1},{1,0},{2,3},{3,2},{4,5},{5,4},{6,7},{7,6},{8,9},{9,8},{10,11... | collective-permute-start | bytes 786440 | tf_op jit(solution)/shard_map/ppermute | solution.py:20
  16.5 18.1 %collective-permute-start.3 = (bf16[128,512]{1,0:T(8,128)(2,1)S(1)}, bf16[128,512]{1,0:T(8,128)(2,1)S(1)}, u32[]{:S(2)}, u32[]{:S(2)}) collective-permute-start(bf16[128,512]{1,0:T(8,128)(2,1)S(1)} %shard_map.56.refs_0_), channel_id=1, source_target_pairs={{0,16},{8,24},{1,17},{9,25},{2,18},{10,26},{3,19},{11,27},{4,20},{... | collective-permute-start | bytes 393224 | tf_op jit(solution)/shard_map/ppermute | solution.py:25
  21.5 13.8 %collective-permute-start.11 = (bf16[128,512]{1,0:T(8,128)(2,1)S(1)}, bf16[128,512]{1,0:T(8,128)(2,1)S(1)}, u32[]{:S(2)}, u32[]{:S(2)}) collective-permute-start(bf16[128,512]{1,0:T(8,128)(2,1)S(1)} %shard_map.57.refs_0_), channel_id=1, source_target_pairs={{0,16},{8,24},{1,17},{9,25},{2,18},{10,26},{3,19},{11,27},{4,20},{... | collective-permute-start | bytes 393224 | tf_op jit(solution)/shard_map/ppermute | solution.py:25
  22.8 13.1 %collective-permute-start.9 = (bf16[128,512]{1,0:T(8,128)(2,1)S(1)}, bf16[128,512]{1,0:T(8,128)(2,1)S(1)}, u32[]{:S(2)}, u32[]{:S(2)}) collective-permute-start(bf16[128,512]{1,0:T(8,128)(2,1)S(1)} %shard_map.56.refs_0_), channel_id=1, source_target_pairs={{0,8},{8,16},{16,24},{1,9},{9,17},{17,25},{2,10},{10,18},{18,26},{... | collective-permute-start | bytes 393224 | tf_op jit(solution)/shard_map/ppermute | solution.py:25
  26.3 11.5 %collective-permute-start.13 = (bf16[128,512]{1,0:T(8,128)(2,1)S(1)}, bf16[128,512]{1,0:T(8,128)(2,1)S(1)}, u32[]{:S(2)}, u32[]{:S(2)}) collective-permute-start(bf16[128,512]{1,0:T(8,128)(2,1)S(1)} %shard_map.57.refs_0_), channel_id=1, source_target_pairs={{0,8},{8,16},{16,24},{1,9},{9,17},{17,25},{2,10},{10,18},{18,26},{... | collective-permute-start | bytes 393224 | tf_op jit(solution)/shard_map/ppermute | solution.py:25
  34.6 5.0 %collective-permute-start.8 = (bf16[128,512]{1,0:T(8,128)(2,1)S(1)}, bf16[128,512]{1,0:T(8,128)(2,1)S(1)}, u32[]{:S(2)}, u32[]{:S(2)}) collective-permute-start(bf16[128,512]{1,0:T(8,128)(2,1)S(1)} %collective-permute-done.3.refs_2_), channel_id=1, source_target_pairs={{16,24},{17,25},{18,26},{19,27},{20,28},{21,29},{22,30},{23,31}} | collective-permute-start | bytes 393224 | tf_op jit(solution)/shard_map/ppermute | solution.py:25
  35.3 5.1 %collective-permute-start.12 = (bf16[128,512]{1,0:T(8,128)(2,1)S(1)}, bf16[128,512]{1,0:T(8,128)(2,1)S(1)}, u32[]{:S(2)}, u32[]{:S(2)}) collective-permute-start(bf16[128,512]{1,0:T(8,128)(2,1)S(1)} %collective-permute-done.11.refs_2_), channel_id=1, source_target_pairs={{16,24},{17,25},{18,26},{19,27},{20,28},{21,29},{22,30},{23,31}} | collective-permute-start | bytes 393224 | tf_op jit(solution)/shard_map/ppermute | solution.py:25
  41.1 15.1 %copy-start = (bf16[1,32,4096]{2,1,0:T(8,128)(2,1)S(1)}, bf16[1,32,4096]{2,1,0:T(8,128)(2,1)}, u32[]{:S(2)}) copy-start(bf16[1,32,4096]{2,1,0:T(8,128)(2,1)} %param.6) | copy-start | bytes 786436
  41.1 2.0 %collective-permute-start.14 = (bf16[64,4096]{1,0:T(8,128)(2,1)S(1)}, bf16[64,4096]{1,0:T(8,128)(2,1)S(1)}, u32[]{:S(2)}, u32[]{:S(2)}) collective-permute-start(bf16[64,4096]{1,0:T(8,128)(2,1)S(1)} %get-tuple-element.42), channel_id=1, source_target_pairs={{0,1},{1,0},{2,3},{3,2},{4,5},{5,4},{6,7},{7,6},{8,9},{9,8},{10,11... | collective-permute-start | bytes 1572872 | tf_op jit(solution)/shard_map/ppermute | solution.py:20
  41.2 4.1 %collective-permute-start.10 = (bf16[64,4096]{1,0:T(8,128)(2,1)S(1)}, bf16[64,4096]{1,0:T(8,128)(2,1)S(1)}, u32[]{:S(2)}, u32[]{:S(2)}) collective-permute-start(bf16[64,4096]{1,0:T(8,128)(2,1)S(1)} %get-tuple-element.35), channel_id=1, source_target_pairs={{0,1},{1,0},{2,3},{3,2},{4,5},{5,4},{6,7},{7,6},{8,9},{9,8},{10,11... | collective-permute-start | bytes 1572872 | tf_op jit(solution)/shard_map/ppermute | solution.py:20
  43.2 6.4 %collective-permute-start.16 = (bf16[32,4096]{1,0:T(8,128)(2,1)S(1)}, bf16[32,4096]{1,0:T(8,128)(2,1)S(1)}, u32[]{:S(2)}, u32[]{:S(2)}) collective-permute-start(bf16[32,4096]{1,0:T(8,128)(2,1)S(1)} %get-tuple-element.44), channel_id=1, source_target_pairs={{0,4},{1,3},{2,6},{3,1},{4,0},{5,7},{6,2},{7,5},{8,12},{9,11},{10,... | collective-permute-start | bytes 786440 | tf_op jit(solution)/shard_map/ppermute | solution.py:20
  45.4 7.5 %collective-permute-start.15 = (bf16[32,4096]{1,0:T(8,128)(2,1)S(1)}, bf16[32,4096]{1,0:T(8,128)(2,1)S(1)}, u32[]{:S(2)}, u32[]{:S(2)}) collective-permute-start(bf16[32,4096]{1,0:T(8,128)(2,1)S(1)} %get-tuple-element.43), channel_id=1, source_target_pairs={{0,4},{1,3},{2,6},{3,1},{4,0},{5,7},{6,2},{7,5},{8,12},{9,11},{10,... | collective-permute-start | bytes 786440 | tf_op jit(solution)/shard_map/ppermute | solution.py:20
  49.7 6.4 %collective-permute-start.17 = (bf16[32,4096]{1,0:T(8,128)(2,1)S(1)}, bf16[32,4096]{1,0:T(8,128)(2,1)S(1)}, u32[]{:S(2)}, u32[]{:S(2)}) collective-permute-start(bf16[32,4096]{1,0:T(8,128)(2,1)S(1)} %fusion), channel_id=1, source_target_pairs={{0,2},{1,5},{2,0},{3,7},{4,6},{5,1},{6,4},{7,3},{8,10},{9,13},{10,... | collective-permute-start | bytes 786440 | tf_op jit(solution)/shard_map/ppermute | solution.py:20
